TPU v7x, 32 devices: a whole 2x2x4 slice. The times are simulated.
32 devices in a mesh: seq: 16 (over z, y, x), head: 2 (over core).
Axes of the slice: x: 2, y: 2, z: 4, core: 2. Of those that a mesh axis runs over, the one named last changes fastest.
Arguments:
- query: bfloat16 [2048, 4096], P('seq', 'head'), may hold values from -20 to 20
- keys: bfloat16 [2048, 4096], P('seq', 'head'), may hold values from -6 to 6
- values: bfloat16 [2048, 4096], P('seq', 'head'), may hold values from -20 to 20
- grad_normed: bfloat16 [2048, 4096], P('seq', 'head'), may hold values from -18 to 18
- norm_gain: float32 [4096], P('head'), may hold values from 0.25 to 1.75
- doc_ids: int32 [2048], P('seq'), may hold values from 0 to 3, never falling along the last dimension, each value on 1 to 1024 neighbouring positions
- home: int32 [2048], P('seq'), may hold values from 0 to 2047, as said below
Outputs:
- input_grads: bfloat16 [2048, 3, 4096], P('seq', None, 'head')
Inputs may be any that keep to these rules, and one draw needn't show every extreme that they name: home is a permutation of 0 to 2047; the owner index along seq of token t is home[t] // 128. Of the 128 tokens on one index of seq, at most 16 have one owner index, and that many is reached for some pairs; every index of seq sends the same multiset of counts to the owners, in a drawn order of owners.
All inputs are finite; a program needn't handle non-finite values.
Results may differ from a plain program's by a relative error of at most 0.0058.
Values may be sent and summed in bfloat16 or wider, within the bound.
A program may use at most 128 MiB of HBM per device.

v0:
```python
import jax
import jax.numpy as jnp
from jax import lax
from jax.sharding import PartitionSpec as P

HEADS = 32
HS = 128


EPSILON = 1e-05
LOW_SENTINEL = -1.0
HIGH_SENTINEL = 1000000000.0


def entering(value, axis, join, neutral, backward):
    count, mine = (lax.axis_size(axis), lax.axis_index(axis))
    pieces = jax.tree.map(lambda part: lax.all_gather(part, axis), value)
    if backward:
        pieces = jax.tree.map(lambda part: part[::-1], pieces)
        mine = count - 1 - mine
    total = jax.tree.map(
        lambda part, zero: jnp.full_like(part, 0) + jnp.asarray(zero, part.dtype), value, neutral
    )

    def step(position, total):
        longer = join(total, jax.tree.map(lambda part: part[position], pieces))
        return jax.tree.map(lambda new, old: jnp.where(position < mine, new, old), longer, total)

    return lax.fori_loop(0, count - 1, step, total)


def masked_scores(left, right, doc_block):
    places = jnp.arange(doc_block.shape[0])
    visible = (doc_block[:, None] == doc_block[None, :]) & (places[:, None] >= places[None, :])
    raw = jnp.einsum("thd,shd->hts", left, right, preferred_element_type=jnp.float32)
    return jnp.where(visible[None], raw, 0.0).astype(jnp.bfloat16)


def outer_sum(left, right, keep):
    kept = jnp.where(keep[:, None, None], left, jnp.zeros_like(left))
    return jnp.einsum("tha,thb->hab", kept, right, preferred_element_type=jnp.float32)


def join_high(earlier, later):
    top = jnp.maximum(earlier[0], later[0])
    state = jnp.where(earlier[0] == top, earlier[1], 0.0) + jnp.where(
        later[0] == top, later[1], 0.0
    )
    return (top, state)


def join_low(earlier, later):
    bottom = jnp.minimum(earlier[0], later[0])
    state = jnp.where(earlier[0] == bottom, earlier[1], 0.0) + jnp.where(
        later[0] == bottom, later[1], 0.0
    )
    return (bottom, state)


def mixed(left, right, form):
    return jnp.einsum(form, left, right, preferred_element_type=jnp.float32)


def local(query, keys, values, grad_normed, norm_gain, doc_ids, home):
    tok_rows, width = query.shape
    heads_here = width // HS
    full_width = HEADS * HS
    query_h = query.reshape(tok_rows, heads_here, HS)
    keys_h = keys.reshape(tok_rows, heads_here, HS)
    values_h = values.reshape(tok_rows, heads_here, HS)
    first_doc = doc_ids[0].astype(jnp.float32)
    last_doc = doc_ids[-1].astype(jnp.float32)
    first_rows = doc_ids == doc_ids[0]
    last_rows = doc_ids == doc_ids[-1]
    first_mask = first_rows[:, None, None]
    last_mask = last_rows[:, None, None]
    attn = masked_scores(query_h, keys_h, doc_ids)
    own_forward = outer_sum(keys_h, values_h, last_rows)
    zero_state = jnp.zeros_like(own_forward)
    into_key, into_state = entering(
        (last_doc, own_forward),
        "seq",
        join_high,
        (jnp.array(LOW_SENTINEL, jnp.float32), zero_state),
        False,
    )
    forward_carry = jnp.where(into_key == first_doc, into_state, 0.0).astype(jnp.bfloat16)
    output = mixed(attn, values_h, "hts,shd->thd") + jnp.where(
        first_mask, mixed(query_h, forward_carry, "tha,hab->thb"), 0.0
    )
    flat = output.reshape(tok_rows, width)
    scaled = norm_gain[None, :] * grad_normed.astype(jnp.float32)
    squares, inner = lax.psum(
        (jnp.sum(flat * flat, axis=1), jnp.sum(scaled * flat, axis=1)), "head"
    )
    inv_rms = lax.rsqrt(squares / full_width + EPSILON)
    grad_out = (
        inv_rms[:, None] * scaled
        - flat * (inv_rms * inv_rms * inv_rms * inner / full_width)[:, None]
    ).astype(jnp.bfloat16)
    grad_h = grad_out.reshape(tok_rows, heads_here, HS)
    back = masked_scores(grad_h, values_h, doc_ids)
    grad_query = mixed(back, keys_h, "hts,shd->thd") + jnp.where(
        first_mask, mixed(grad_h, forward_carry, "thb,hab->tha"), 0.0
    )
    grad_query = grad_query.astype(jnp.bfloat16).reshape(tok_rows, width)
    own_reverse = outer_sum(query_h, grad_h, first_rows)
    seq_count = lax.axis_size("seq")
    capacity = 2 * tok_rows // seq_count
    owner = home // tok_rows
    target_row = home % tok_rows
    places = jnp.arange(tok_rows)
    chosen = (owner[:, None] == jnp.arange(seq_count)[None, :]).astype(jnp.bfloat16)
    earlier_rows = (places[:, None] > places[None, :]).astype(jnp.bfloat16)
    before = jnp.dot(earlier_rows, chosen, preferred_element_type=jnp.float32)
    ranks = jnp.sum(before * chosen.astype(jnp.float32), axis=1).astype(jnp.int32)
    row_index = (
        jnp.full((seq_count, capacity), tok_rows, jnp.int32).at[owner, ranks].set(target_row)
    )
    back_key, back_state = entering(
        (first_doc, own_reverse),
        "seq",
        join_low,
        (jnp.array(HIGH_SENTINEL, jnp.float32), zero_state),
        True,
    )
    reverse_carry = jnp.where(back_key == last_doc, back_state, 0.0).astype(jnp.bfloat16)
    grad_keys = mixed(back, query_h, "hts,thd->shd") + jnp.where(
        last_mask, mixed(values_h, reverse_carry, "thb,hab->tha"), 0.0
    )
    grad_values = mixed(attn, grad_h, "hts,thd->shd") + jnp.where(
        last_mask, mixed(keys_h, reverse_carry, "tha,hab->thb"), 0.0
    )
    pair = jnp.stack(
        [
            grad_keys.astype(jnp.bfloat16).reshape(tok_rows, width),
            grad_values.astype(jnp.bfloat16).reshape(tok_rows, width),
        ],
        axis=1,
    )
    stacked = jnp.concatenate([grad_query[:, None, :], pair], axis=1)
    bucket = jnp.zeros((seq_count, capacity, 3, width), jnp.bfloat16).at[owner, ranks].set(stacked)
    received, index_back = (
        lax.all_to_all(bucket, "seq", split_axis=0, concat_axis=0, tiled=True),
        lax.all_to_all(row_index, "seq", split_axis=0, concat_axis=0, tiled=True),
    )
    result = jnp.zeros((tok_rows, 3, width), jnp.bfloat16)
    return result.at[index_back.reshape(-1)].set(received.reshape(-1, 3, width), mode="drop")


def solution(mesh):
    placed = (
        P("seq", "head"),
        P("seq", "head"),
        P("seq", "head"),
        P("seq", "head"),
        P("head"),
        P("seq"),
        P("seq"),
    )
    return jax.shard_map(
        local, mesh=mesh, in_specs=placed, out_specs=P("seq", None, "head"), check_vma=False
    )
```

profile of v0, /device:TPU:0, one launch (start us, length us, event | category | flops | bytes accessed | tf_op | source)
XLA Modules:
  0.0 683.8 jit_solution(3932278371381121612)
XLA Ops:
  6.6 1.4 fusion.48
  9.6 1.9 broadcast_compare_fusion.1
  16.6 44.4 %all-reduce.2 = (f32[16]{0:T(128)S(1)}, f32[16]{0:T(128)S(1)}) all-reduce(f32[16]{0:T(128)S(1)} %dynamic-update-slice.1, f32[16]{0:T(128)S(1)} %dynamic-update-slice), channel_id=1, replica_groups=mesh['seq'=16,'head'=2] {'seq'}, use_global_device_ids=true, to_apply=%add.1 | all-reduce | flops 32 | bytes 256
  61.1 1.4 fusion.8
  62.4 145.4 %all-gather.5.cloned.1.call-done = f32[256,128,128]{2,1,0:T(8,128)} async-done(((f32[16,128,128]{2,1,0:T(8,128)}), f32[256,128,128]{2,1,0:T(8,128)}) %all-gather.5.cloned.1.call-update) | async-done | bytes 16777232 | tf_op jit(solution)/shard_map/all_gather | solution.py:17
  207.8 56.7 %while.32 = (s32[]{:T(128)}, f32[]{:T(128)}, f32[16,128,128]{2,1,0:T(8,128)S(1)}, s32[]{:T(128)}, f32[16]{0:T(128)S(1)}, /*index=5*/f32[16,16,128,128]{3,2,1,0:T(8,128)}, s32[]{:T(128)}, s32[]{:T(128)}) while((s32[]{:T(128)}, f32[]{:T(128)}, f32[16,128,128]{2,1,0:T(8,128)S(1)}, s32[]{:T(128)}, f32[16]{0:T(128)S(1)}, ...), condition=%wide.region_3.4_spmd.clone, body=%wide.region_2.3_spmd.clone.sunk | while | flops 1310728 | bytes 3145894 | solution.py:29
  209.7 1.9 fusion.69
  213.5 1.9 fusion.69
  217.2 1.9 fusion.69
  221.0 1.9 fusion.69
  224.8 1.9 fusion.69
  228.6 1.9 fusion.69
  232.4 1.9 fusion.69
  236.1 1.9 fusion.69
  239.9 1.9 fusion.69
  243.7 1.9 fusion.69
  247.5 1.9 fusion.69
  251.3 1.9 fusion.69
  255.0 1.9 fusion.69
  258.8 1.9 fusion.69
  262.6 1.9 fusion.69
  264.9 2.5 multiply_reduce_fusion.1
  267.3 1.6 copy.87
  268.9 1.3 multiply_reduce_fusion
  270.2 2.5 all-reduce.3
  272.7 2.1 subtract_convert_fusion
  274.7 1.3 copy.109
  276.0 1.5 fusion.21
  278.3 17.9 %scatter_fusion = s32[16,16]{1,0:T(8,128)} fusion(s32[16,16]{1,0:T(8,128)} %broadcast_in_dim.115, s32[128]{0:T(128)S(1)} %fusion.41, s32[128]{0:T(128)S(1)} %get-tuple-element.305), kind=kCustom, calls=%fused_computation | custom fusion | bytes 2560 | tf_op jit(solution)/shard_map/scatter | solution.py:118
  296.3 4.1 all-to-all-start
  300.6 1.6 fusion.9
  302.2 1.5 fusion.3
  304.2 2.1 copy.99
  306.3 161.3 %all-gather.7.cloned.1.call-done = f32[256,128,128]{2,1,0:T(8,128)} async-done(((f32[16,128,128]{2,1,0:T(8,128)}), f32[256,128,128]{2,1,0:T(8,128)}) %all-gather.7.cloned.1.call-update) | async-done | bytes 16777232 | tf_op jit(solution)/shard_map/all_gather | solution.py:17
  467.6 11.6 %rev.7 = f32[16,16,128,128]{3,2,1,0:T(8,128)} reverse(f32[16,16,128,128]{3,2,1,0:T(8,128)} %bitcast.122), dimensions={0} | reverse | bytes 33554432 | tf_op jit(solution)/shard_map/rev | solution.py:19
  479.3 56.7 %while.33 = (s32[]{:T(128)}, f32[]{:T(128)}, f32[16,128,128]{2,1,0:T(8,128)S(1)}, s32[]{:T(128)}, f32[16]{0:T(128)S(1)}, /*index=5*/f32[16,16,128,128]{3,2,1,0:T(8,128)}, s32[]{:T(128)}, s32[]{:T(128)}) while((s32[]{:T(128)}, f32[]{:T(128)}, f32[16,128,128]{2,1,0:T(8,128)S(1)}, s32[]{:T(128)}, f32[16]{0:T(128)S(1)}, ...), condition=%wide.region_9.10_spmd.clone, body=%wide.region_8.9_spmd.clone.sunk | while | flops 1310728 | bytes 3145894 | solution.py:29
  481.2 1.9 fusion.70
  484.9 1.9 fusion.70
  488.7 1.9 fusion.70
  492.5 1.9 fusion.70
  496.3 1.9 fusion.70
  500.1 1.9 fusion.70
  503.8 1.9 fusion.70
  507.6 1.9 fusion.70
  511.4 1.9 fusion.70
  515.2 1.9 fusion.70
  519.0 1.9 fusion.70
  522.7 1.9 fusion.70
  526.5 1.9 fusion.70
  530.3 1.9 fusion.70
  534.1 1.9 fusion.70
  536.5 2.5 convolution_select_fusion
  539.3 2.0 copy.100
  541.3 1.7 fusion.11
  544.0 5.7 pad_maximum_fusion
  549.7 4.1 broadcast_in_dim.117
  553.7 19.1 %scatter_fusion.1 = bf16[16,16,3,2048]{3,2,1,0:T(4,128)(2,1)} fusion(bf16[16,16,3,2048]{3,2,1,0:T(4,128)(2,1)} %broadcast_in_dim.117, s32[128]{0:T(128)S(1)} %fusion.41, bf16[128,3,2048]{2,1,0:T(4,128)(2,1)} %pad_maximum_fusion), kind=kCustom, calls=%fused_computation.1 | custom fusion | bytes 4719616 | tf_op jit(solution)/shard_map/scatter | solution.py:142
  572.8 6.4 copy.102
  579.2 4.7 all-to-all-start.1
  585.2 59.3 %all-to-all-done.1 = bf16[16,16,3,2048]{3,1,2,0:T(8,128)(2,1)} async-done(((bf16[16,16,3,2048]{3,1,2,0:T(8,128)(2,1)}), bf16[16,16,3,2048]{3,1,2,0:T(8,128)(2,1)}, u32[]{:S(2)}, u32[]{:S(2)}) %all-to-all-start.1) | async-done | bytes 3145760 | tf_op jit(solution)/shard_map/all_to_all | solution.py:144
  644.5 2.1 copy.103
  646.6 4.6 copy.104
  652.3 22.3 %scatter_fusion.2 = bf16[128,3,2048]{2,1,0:T(4,128)(2,1)S(1)} fusion(bf16[128,3,2048]{2,1,0:T(4,128)(2,1)S(1)} %broadcast_in_dim.114, s32[256]{0:T(256)S(1)} %bitcast.139, bf16[256,3,2048]{2,1,0:T(4,128)(2,1)} %copy.104), kind=kCustom, calls=%fused_computation.2 | custom fusion | bytes 9438208 | tf_op jit(solution)/shard_map/scatter | solution.py:148
  674.6 2.3 copy.105
  (93 shorter events, 29.0 us)
Async XLA Ops:
  6.5 4.9 copy-start
  6.5 7.8 %copy-start.14 = (u32[32]{0:T(128)S(1)}, u32[32]{0:T(128)}, u32[]{:S(2)}) copy-start(u32[32]{0:T(128)} %constant.150) | copy-start | bytes 388
  6.5 54.5 %copy-start.12 = (s32[128]{0:T(128)S(1)}, s32[128]{0:T(128)}, u32[]{:S(2)}) copy-start(s32[128]{0:T(128)} %param.16) | copy-start | bytes 1540
  6.5 54.5 %copy-start.9 = (bf16[128,2048]{1,0:T(8,128)(2,1)S(1)}, bf16[128,2048]{1,0:T(8,128)(2,1)}, u32[]{:S(2)}) copy-start(bf16[128,2048]{1,0:T(8,128)(2,1)} %param.12) | copy-start | bytes 1572868
  6.5 7.5 %copy-start.10 = (bf16[128,2048]{1,0:T(8,128)(2,1)S(1)}, bf16[128,2048]{1,0:T(8,128)(2,1)}, u32[]{:S(2)}) copy-start(bf16[128,2048]{1,0:T(8,128)(2,1)} %param.11) | copy-start | bytes 1572868
  6.5 201.2 %all-gather.5.cloned.1.call-start = ((), (), s32[]{:S(2)}) async-start(), calls=%async_computation.2 | async-start | bytes 17825792 | tf_op jit(solution)/shard_map/all_gather | solution.py:17
  9.6 3.8 copy-start.4
  12.8 454.9 %all-gather.7.cloned.1.call-start = ((), (), s32[]{:S(2)}) async-start(), calls=%async_computation.3 | async-start | bytes 17825792 | tf_op jit(solution)/shard_map/all_gather | solution.py:17
  264.5 4.4 copy-start.11
  268.9 8.6 %copy-start.13 = (s32[128]{0:T(128)S(1)}, s32[128]{0:T(128)}, u32[]{:S(2)}) copy-start(s32[128]{0:T(128)} %param.17) | copy-start | bytes 1540
  276.0 1.5 copy-start.2
  296.3 282.9 %all-to-all-start = ((s32[16,1,16]{2,1,0:T(1,128)}), s32[16,1,16]{2,1,0:T(1,128)S(1)}, u32[]{:S(2)}, u32[]{:S(2)}) async-start(s32[16,1,16]{2,1,0:T(1,128)} %bitcast.4), calls=%async_computation | async-start | bytes 16384 | tf_op jit(solution)/shard_map/all_to_all | solution.py:145
  300.6 3.2 copy-start.5
  302.2 2.0 copy-start.7
  536.0 3.1 copy-start.8
  536.0 5.4 copy-start.3
  539.0 5.0 copy-start.6
  579.2 65.3 %all-to-all-start.1 = ((bf16[16,16,3,2048]{3,1,2,0:T(8,128)(2,1)}), bf16[16,16,3,2048]{3,1,2,0:T(8,128)(2,1)}, u32[]{:S(2)}, u32[]{:S(2)}) async-start(bf16[16,16,3,2048]{3,1,2,0:T(8,128)(2,1)} %copy.102), calls=%async_computation.1 | async-start | bytes 6291456 | tf_op jit(solution)/shard_map/all_to_all | solution.py:144
  652.3 24.6 %copy-start.1 = (bf16[128,2048]{1,0:T(8,128)(2,1)S(1)}, bf16[128,2048]{1,0:T(8,128)(2,1)}, u32[]{:S(2)}) copy-start(bf16[128,2048]{1,0:T(8,128)(2,1)} %param.13) | copy-start | bytes 1572868
Sparse Core Ops, SparseCore 0:
  12.9 194.8 all-gather.4
  277.6 189.9 all-gather.6
where the time goes:
time: 696 us; the launch traced here: 684 us
  waiting for transfers between devices  366 us (53%)
  local copies, waits for them, and re-layouts  124 us (18%)
  other arithmetic  67.5 us (10%)
  blocking collectives  46.8 us (7%)
  loops' own time  39.9 us (6%)
  matrix products  15.7 us (2%)
  between operations  15 us (2%)
  starting transfers between devices  8.93 us (1%)
    all_gather x2, waiting for transfers between devices, entering(): pieces = jax.tree.map(lambda part: lax.all_gather(part, axis), value)  307 us
    all_to_all x1, waiting for transfers between devices, local(): lax.all_to_all(bucket, 'seq', split_axis=0, concat_axis=0, tiled=True)  59.3 us
    select_n x30, other arithmetic, step(): jnp.where(position < mine, new, old)  55.9 us
    unnamed x1, blocking collectives  44.4 us
    another operation x2, loops' own time, entering(): return lax.fori_loop(0, count - 1, step, total)  39.9 us
    scatter x2, local copies, waits for them, and re-layouts, local(): jnp.zeros((seq_count, capacity, 3, width), jnp.bfloat16).at[owner, ranks]  25.4 us
    scatter x2, local copies, waits for them, and re-layouts, local(): result.at[index_back.reshape(-1)]  24.6 us
    scatter x1, local copies, waits for them, and re-layouts, local(): jnp.full((seq_count, capacity), tok_rows, jnp.int32).at[owner, ranks]  17.9 us
  transfers between devices with their start and end apart: 4, of which 3 were waited for; matrix products, arithmetic and copies ran while one was open for 18% of the time, Pallas kernels for 0%

commit v1 on v0

v1 whole, which is shorter than its diff:
```python
import functools

import jax
import jax.numpy as jnp
from jax import lax
from jax.experimental import pallas as pl
from jax.experimental.pallas import tpu as pltpu
from jax.sharding import PartitionSpec as P

HEADS = 32
HS = 128
EPSILON = 1e-05
GROUP = 4
F32 = jnp.float32
BF16 = jnp.bfloat16


def dot(left, right, left_dim, right_dim):
    return lax.dot_general(
        left, right, (((left_dim,), (right_dim,)), ((), ())), preferred_element_type=F32
    )


def rows_at(index, size):
    return pl.ds(pl.multiple_of(index * size, size), size)


def kernel(
    n, nh, chunk, cap,
    q_ref, k_ref, v_ref, gn_ref, gain_ref, meta_ref,
    out_ref,
    metas, fw_own, fw_in, fw_send, fw_carry, rv_own, rv_in, rv_send, rv_carry,
    attn_ref, back_ref, o_ref, go_ref, gk_ref, gv_ref, sums_out, sums_in,
    pack_ref, unpack_ref, bq_send, bq_in, bkv_send, bkv_in,
    sem_send, sem_recv, sum_send, sum_recv,
):
    tok, width = q_ref.shape
    heads = width // HS
    me = lax.axis_index("seq")
    me_head = lax.axis_index("head")

    barrier = pltpu.get_barrier_semaphore()

    def greet(step, _):
        pl.semaphore_signal(
            barrier, inc=1, device_id={"seq": lax.rem(me + step, n)},
            device_id_type=pl.DeviceIdType.MESH,
        )
        return 0

    def greet_head(step, _):
        pl.semaphore_signal(
            barrier, inc=1, device_id={"head": lax.rem(me_head + step, nh)},
            device_id_type=pl.DeviceIdType.MESH,
        )
        return 0

    lax.fori_loop(1, n, greet, 0)
    lax.fori_loop(1, nh, greet_head, 0)

    def remote(which, src, dst, rows, to, slot, whole_src=False):
        return pltpu.make_async_remote_copy(
            src_ref=src if whole_src else src.at[rows_at(to, rows)],
            dst_ref=dst.at[rows_at(slot, rows)],
            send_sem=sem_send.at[which, to],
            recv_sem=sem_recv.at[which, slot],
            device_id={"seq": to},
            device_id_type=pl.DeviceIdType.MESH,
        )

    def start(which, src, dst, rows, whole_src=False):
        def body(step, _):
            remote(which, src, dst, rows, lax.rem(me + step, n), me, whole_src).start()
            return 0

        lax.fori_loop(1, n, body, 0)

    def finish_recv(which, src, dst, rows, whole_src=False):
        def body(step, _):
            other = lax.rem(me + step, n)
            remote(which, src, dst, rows, other, other, whole_src).wait_recv()
            return 0

        lax.fori_loop(1, n, body, 0)

    def finish_send(which, src, dst, rows, whole_src=False):
        def body(step, _):
            remote(which, src, dst, rows, lax.rem(me + step, n), me, whole_src).wait_send()
            return 0

        lax.fori_loop(1, n, body, 0)

    def each_head(body):
        group = GROUP if heads % GROUP == 0 else 1

        def outer(index, _):
            for inner in range(group):
                head = index * group + inner
                body(head, rows_at(head, HS))
            return 0

        lax.fori_loop(0, heads // group, outer, 0)

    doc_row = jnp.broadcast_to(meta_ref[4:5, :], (tok, tok))
    doc_col = doc_row.T
    first_doc, last_doc = meta_ref[2:3, :], meta_ref[3:4, :]
    place_row = lax.broadcasted_iota(jnp.int32, (tok, tok), 0)
    place_col = lax.broadcasted_iota(jnp.int32, (tok, tok), 1)
    visible = (doc_col == doc_row) & (place_col <= place_row)
    first_mask = doc_col == first_doc
    last_mask = doc_col == last_doc
    before = jnp.where(place_row < place_col, 1.0, 0.0).astype(BF16)

    def own_forward(head, at):
        kept = jnp.where(last_mask, k_ref[:, at].astype(F32), 0.0).astype(BF16)
        fw_own[at, :] = dot(kept, v_ref[:, at], 0, 0).astype(BF16)

    if n * chunk > heads * HS:
        fw_own[heads * HS :, :] = jnp.zeros((n * chunk - heads * HS, HS), BF16)
        rv_own[heads * HS :, :] = jnp.zeros((n * chunk - heads * HS, HS), BF16)
    each_head(own_forward)
    metas[rows_at(me, 8), :] = meta_ref[...]
    fw_in[rows_at(me, chunk), :] = fw_own[rows_at(me, chunk), :]
    pl.semaphore_wait(barrier, (n - 1) + (nh - 1))
    start(0, meta_ref, metas, 8, True)
    start(1, fw_own, fw_in, chunk)

    def inside(head, at):
        attn = jnp.where(visible, dot(q_ref[:, at], k_ref[:, at], 1, 1), 0.0).astype(BF16)
        attn_ref[at, :] = attn
        o_ref[:, at] = dot(attn, v_ref[:, at], 1, 0)

    each_head(inside)

    slots = lax.broadcasted_iota(jnp.int32, (cap, tok), 0).astype(F32)
    lanes = lax.broadcasted_iota(jnp.int32, (cap, tok), 1).astype(F32)

    def picks(owners, owner):
        chosen = jnp.broadcast_to(jnp.where(owners == owner, 1.0, 0.0), (cap, tok))
        rank = dot(chosen.astype(BF16), before, 1, 0)
        return jnp.where(rank == slots, chosen, 0.0)

    def pack(owner, _):
        pack_ref[rows_at(owner, cap), :] = picks(meta_ref[0:1, :], owner.astype(F32)).astype(BF16)
        return 0

    lax.fori_loop(0, n, pack, 0)

    finish_recv(0, meta_ref, metas, 8, True)
    finish_recv(1, fw_own, fw_in, chunk)

    def doc(block, which):
        return metas[pl.ds(block * 8 + which, 1), :]

    fw_send[rows_at(0, chunk), :] = jnp.zeros((chunk, HS), BF16)

    def forward_step(block, total):
        total = fw_in[rows_at(block - 1, chunk), :].astype(F32) + total
        met = jnp.where(doc(block, 2) == doc(block - 1, 3), 1.0, 0.0)
        fw_send[rows_at(block, chunk), :] = (total * met).astype(BF16)
        return total * jnp.where(doc(block, 3) == doc(block - 1, 3), 1.0, 0.0)

    lax.fori_loop(1, n, forward_step, jnp.zeros((chunk, HS), F32))
    start(2, fw_send, fw_carry, chunk)
    fw_carry[rows_at(me, chunk), :] = fw_send[rows_at(me, chunk), :]

    def unpack(source, _):
        chosen = picks(metas[pl.ds(source * 8, 1), :], me.astype(F32))
        row = jnp.sum(chosen * metas[pl.ds(source * 8 + 1, 1), :], axis=1, keepdims=True)
        used = jnp.sum(chosen, axis=1, keepdims=True)
        unpack_ref[rows_at(source, cap), :] = (
            jnp.where(row == lanes, 1.0, 0.0) * used
        ).astype(BF16)
        return 0

    lax.fori_loop(0, n, unpack, 0)
    finish_recv(2, fw_send, fw_carry, chunk)

    def output(head, at):
        add = dot(q_ref[:, at], fw_carry[at, :], 1, 0)
        total = o_ref[:, at] + jnp.where(first_mask, add, 0.0)
        o_ref[:, at] = total
        scaled = gain_ref[:, at] * gn_ref[:, at].astype(F32)
        return total * total, scaled * total

    squares = jnp.zeros((tok, HS), F32)
    inner = jnp.zeros((tok, HS), F32)

    group = GROUP if heads % GROUP == 0 else 1

    def output_step(index, sums):
        squares, inner = sums
        for part in range(group):
            head = index * group + part
            one, two = output(head, rows_at(head, HS))
            squares, inner = squares + one, inner + two
        return squares, inner

    squares, inner = lax.fori_loop(0, heads // group, output_step, (squares, inner))
    squares = jnp.sum(squares, axis=1, keepdims=True)
    inner = jnp.sum(inner, axis=1, keepdims=True)
    pair = jnp.where(place_col < HS // 2, squares, inner)
    sums_out[...] = pair

    def sum_copy(to, slot):
        return pltpu.make_async_remote_copy(
            src_ref=sums_out,
            dst_ref=sums_in.at[rows_at(slot, tok)],
            send_sem=sum_send.at[to],
            recv_sem=sum_recv.at[slot],
            device_id={"head": to},
            device_id_type=pl.DeviceIdType.MESH,
        )

    def sum_start(step, _):
        sum_copy(lax.rem(me_head + step, nh), me_head).start()
        return 0

    def sum_finish(step, total):
        other = lax.rem(me_head + step, nh)
        sum_copy(other, other).wait_recv()
        return total + sums_in[rows_at(other, tok), :]

    def sum_sent(step, _):
        sum_copy(lax.rem(me_head + step, nh), me_head).wait_send()
        return 0

    lax.fori_loop(1, nh, sum_start, 0)
    pair = lax.fori_loop(1, nh, sum_finish, pair)
    full = HEADS * HS
    inv_rms = lax.rsqrt(pair[:, 0:1] / full + EPSILON)
    pull = inv_rms * inv_rms * inv_rms * pair[:, HS - 1 : HS] / full
    inv_rms = jnp.broadcast_to(inv_rms, (tok, HS))
    pull = jnp.broadcast_to(pull, (tok, HS))

    def own_reverse(head, at):
        scaled = gain_ref[:, at] * gn_ref[:, at].astype(F32)
        grad = (inv_rms * scaled - o_ref[:, at] * pull).astype(BF16)
        go_ref[:, at] = grad
        kept = jnp.where(first_mask, q_ref[:, at].astype(F32), 0.0).astype(BF16)
        rv_own[at, :] = dot(kept, grad, 0, 0).astype(BF16)

    each_head(own_reverse)
    start(3, rv_own, rv_in, chunk)
    rv_in[rows_at(me, chunk), :] = rv_own[rows_at(me, chunk), :]

    def grad_query(head, at):
        grad = go_ref[:, at]
        back = jnp.where(visible, dot(grad, v_ref[:, at], 1, 1), 0.0).astype(BF16)
        back_ref[at, :] = back
        add = dot(grad, fw_carry[at, :], 1, 1)
        result = dot(back, k_ref[:, at], 1, 0) + jnp.where(first_mask, add, 0.0)
        bq_send[:, at] = dot(pack_ref[...], result.astype(BF16), 1, 0).astype(BF16)

    each_head(grad_query)
    bq_in[rows_at(me, cap), :] = bq_send[rows_at(me, cap), :]
    start(5, bq_send, bq_in, cap)

    finish_recv(3, rv_own, rv_in, chunk)
    rv_send[rows_at(n - 1, chunk), :] = jnp.zeros((chunk, HS), BF16)

    def reverse_step(step, total):
        block = n - 1 - step
        total = rv_in[rows_at(block + 1, chunk), :].astype(F32) + total
        met = jnp.where(doc(block, 3) == doc(block + 1, 2), 1.0, 0.0)
        rv_send[rows_at(block, chunk), :] = (total * met).astype(BF16)
        return total * jnp.where(doc(block, 2) == doc(block + 1, 2), 1.0, 0.0)

    lax.fori_loop(1, n, reverse_step, jnp.zeros((chunk, HS), F32))
    start(4, rv_send, rv_carry, chunk)
    rv_carry[rows_at(me, chunk), :] = rv_send[rows_at(me, chunk), :]

    def inside_back(head, at):
        gk_ref[:, at] = dot(back_ref[at, :], q_ref[:, at], 0, 0)
        gv_ref[:, at] = dot(attn_ref[at, :], go_ref[:, at], 0, 0)

    each_head(inside_back)
    finish_recv(4, rv_send, rv_carry, chunk)

    def grad_pair(head, at):
        carry = rv_carry[at, :]
        key = gk_ref[:, at] + jnp.where(last_mask, dot(v_ref[:, at], carry, 1, 1), 0.0)
        value = gv_ref[:, at] + jnp.where(last_mask, dot(k_ref[:, at], carry, 1, 0), 0.0)
        bkv_send[:, at] = dot(pack_ref[...], key.astype(BF16), 1, 0).astype(BF16)
        bkv_send[:, rows_at(head + heads, HS)] = dot(
            pack_ref[...], value.astype(BF16), 1, 0
        ).astype(BF16)

    each_head(grad_pair)
    start(6, bkv_send, bkv_in, cap)
    bkv_in[rows_at(me, cap), :] = bkv_send[rows_at(me, cap), :]

    finish_recv(5, bq_send, bq_in, cap)

    def place_query(head, at):
        out_ref[:, at] = dot(unpack_ref[...], bq_in[:, at], 0, 0).astype(BF16)

    each_head(place_query)
    finish_recv(6, bkv_send, bkv_in, cap)

    def place_pair(head, at):
        for part in range(2):
            out_ref[:, rows_at(head + (part + 1) * heads, HS)] = dot(
                unpack_ref[...], bkv_in[:, rows_at(head + part * heads, HS)], 0, 0
            ).astype(BF16)

    each_head(place_pair)

    finish_send(0, meta_ref, metas, 8, True)
    finish_send(1, fw_own, fw_in, chunk)
    finish_send(2, fw_send, fw_carry, chunk)
    lax.fori_loop(1, nh, sum_sent, 0)
    finish_send(3, rv_own, rv_in, chunk)
    finish_send(4, rv_send, rv_carry, chunk)
    finish_send(5, bq_send, bq_in, cap)
    finish_send(6, bkv_send, bkv_in, cap)


def local(n, nh, query, keys, values, grad_normed, norm_gain, doc_ids, home):
    tok, width = query.shape
    heads = width // HS
    chunk = max(16, heads * HS // n)
    cap = max(16, 2 * tok // n)
    rows = jnp.stack(
        [
            home // tok,
            home % tok,
            jnp.broadcast_to(doc_ids[0], (tok,)),
            jnp.broadcast_to(doc_ids[-1], (tok,)),
            doc_ids,
        ]
    ).astype(F32)
    meta = jnp.concatenate([rows, jnp.zeros((3, tok), F32)], axis=0)
    states = pltpu.VMEM((n * chunk, HS), BF16)
    scores = pltpu.VMEM((heads * HS, HS), BF16)
    wide = pltpu.VMEM((tok, width), F32)
    vmem = pl.BlockSpec(memory_space=pltpu.VMEM)
    result = pl.pallas_call(
        functools.partial(kernel, n, nh, chunk, cap),
        out_shape=jax.ShapeDtypeStruct((tok, 3 * width), BF16),
        in_specs=[vmem] * 6,
        out_specs=vmem,
        scratch_shapes=[
            pltpu.VMEM((n * 8, tok), F32),
            states, states, states, states, states, states, states, states,
            scores, scores,
            wide,
            pltpu.VMEM((tok, width), BF16),
            wide, wide,
            pltpu.VMEM((tok, HS), F32),
            pltpu.VMEM((nh * tok, HS), F32),
            pltpu.VMEM((n * cap, tok), BF16),
            pltpu.VMEM((n * cap, tok), BF16),
            pltpu.VMEM((n * cap, width), BF16),
            pltpu.VMEM((n * cap, width), BF16),
            pltpu.VMEM((n * cap, 2 * width), BF16),
            pltpu.VMEM((n * cap, 2 * width), BF16),
            pltpu.SemaphoreType.DMA((7, n)),
            pltpu.SemaphoreType.DMA((7, n)),
            pltpu.SemaphoreType.DMA((nh,)),
            pltpu.SemaphoreType.DMA((nh,)),
        ],
        compiler_params=pltpu.CompilerParams(
            collective_id=0, has_side_effects=True, vmem_limit_bytes=48 * 1024 * 1024
        ),
    )(query, keys, values, grad_normed, norm_gain[None, :], meta)
    return result.reshape(tok, 3, width)


def solution(mesh):
    placed = (
        P("seq", "head"),
        P("seq", "head"),
        P("seq", "head"),
        P("seq", "head"),
        P("head"),
        P("seq"),
        P("seq"),
    )
    return jax.shard_map(
        functools.partial(local, mesh.shape["seq"], mesh.shape["head"]),
        mesh=mesh, in_specs=placed, out_specs=P("seq", None, "head"), check_vma=False,
    )
```

time: 696 us -> 153 us (0.22)
  the two profiles are of different devices: /device:TPU:0 before, /device:TPU:31 now
where the time goes in v1:
time: 153 us; the launch traced here: 152 us
  Pallas kernels  141 us (92%)
  local copies, waits for them, and re-layouts  10.7 us (7%)
    pallas_call x1, Pallas kernels, local(): pl.pallas_call(functools.partial(kernel, n, nh, chunk, cap), out_shape=ja...  141 us
    unnamed x10, local copies, waits for them, and re-layouts  4.86 us

profile of v1, /device:TPU:31, one launch (start us, length us, event | category | flops | bytes accessed | tf_op | source)
XLA Modules:
  0.0 152.3 jit_solution(4168836470709850791)
XLA Ops:
  0.0 0.7 fusion
  0.7 1.3 fusion.2
  2.0 0.6 stack_broadcast_in_dim.7
  2.6 0.7 stack_broadcast_in_dim.6
  3.3 0.7 stack.15
  4.0 0.0 copy-start
  4.0 1.0 copy-done
  5.1 0.0 copy-start.1
  5.1 1.0 copy-done.1
  6.1 0.0 copy-start.2
  6.1 1.0 copy-done.2
  7.2 0.0 copy-start.3
  7.2 1.0 copy-done.3
  8.2 0.0 copy-start.4
  8.2 0.7 copy-done.4
  8.9 140.9 %shard_map.73 = bf16[128,6144]{1,0:T(8,128)(2,1)S(1)} custom-call(bf16[128,2048]{1,0:T(8,128)(2,1)S(1)} %copy-done, bf16[128,2048]{1,0:T(8,128)(2,1)S(1)} %copy-done.1, bf16[128,2048]{1,0:T(8,128)(2,1)S(1)} %copy-done.2, bf16[128,2048]{1,0:T(8,128)(2,1)S(1)} %copy-done.3, f32[1,2048]{1,0:T(1,128)S(1)} %bitcast.9, f32[8,128]{1,0:T(8,128)S(1)} %concatenate.3.meta_ref), custom_call_target="tpu_custom_call" | custom-call | tf_op jit(solution)/shard_map/pallas_call | solution.py:338
  149.8 0.9 copy.9
  150.7 1.6 %copy.10 = bf16[128,3,2048]{2,0,1:T(8,128)(2,1)} copy(bf16[128,3,2048]{0,2,1:T(8,128)(2,1)S(1)} %bitcast.10) | data formatting | bytes 3145728 | tf_op jit(solution)/shard_map/reshape | solution.py:367
  (2 shorter events, 0.0 us)
Async XLA Ops:
  4.0 1.0 copy-start
  5.1 1.0 copy-start.1
  6.1 1.0 copy-start.2
  7.2 1.0 copy-start.3
  8.2 0.7 copy-start.4

commit v2 on v1

v2 whole, which is shorter than its diff:
```python
import functools

import jax
import jax.numpy as jnp
from jax import lax
from jax.experimental import pallas as pl
from jax.experimental.pallas import tpu as pltpu
from jax.sharding import PartitionSpec as P

HEADS = 32
HS = 128
EPSILON = 1e-05
PLANE = 4
SUBS = 4
F32 = jnp.float32
BF16 = jnp.bfloat16


def dot(left, right, left_dim, right_dim):
    return lax.dot_general(
        left, right, (((left_dim,), (right_dim,)), ((), ())), preferred_element_type=F32
    )


def rows_at(index, size):
    return pl.ds(pl.multiple_of(index * size, size), size)


MESH = pl.DeviceIdType.MESH


def rows_from(offset, size):
    return pl.ds(pl.multiple_of(offset, size), size)


def same(left, right):
    return jnp.where(left == right, 1.0, 0.0)


def kernel(
    n, nh, cap,
    q_hbm, k_hbm, v_hbm, gn_hbm, gain_hbm, doc_hbm, home_hbm,
    out_ref,
    q_ref, k_ref, v_ref, gn_ref, gain_ref, doc_ref, home_ref,
    meta_ref, metas,
    fw_own, fw_in, fw_total, fw_far, fw_send, fw_carry,
    rv_own, rv_in, rv_total, rv_far, rv_send, rv_carry,
    attn_ref, back_ref, o_ref, go_ref, gk_ref, gv_ref, sums_out, sums_in,
    pack_ref, unpack_ref, bq_send, bq_in, bkv_send, bkv_in,
    in_sem, meta_sems, near_sems, far_sems, carry_sems, q_sems, kv_sems, sum_sems,
):
    tok, width = q_ref.shape
    heads = width // HS
    quarter = heads * HS // PLANE
    sub = quarter // SUBS
    aligned = sub == HS
    each = heads // SUBS
    planes = n // PLANE
    me = lax.axis_index("seq")
    me_head = lax.axis_index("head")
    plane, spot = me // PLANE, lax.rem(me, PLANE)

    loads = [
        pltpu.make_async_copy(src, dst, in_sem.at[index])
        for index, (src, dst) in enumerate(
            [
                (doc_hbm, doc_ref), (home_hbm, home_ref), (k_hbm, k_ref), (v_hbm, v_ref),
                (q_hbm, q_ref), (gn_hbm, gn_ref), (gain_hbm, gain_ref),
            ]
        )
    ]
    for load in loads:
        load.start()

    barrier = pltpu.get_barrier_semaphore()

    def greet(step, _):
        pl.semaphore_signal(
            barrier, inc=1, device_id={"seq": lax.rem(me + step, n)}, device_id_type=MESH
        )
        return 0

    def greet_head(step, _):
        pl.semaphore_signal(
            barrier, inc=1, device_id={"head": lax.rem(me_head + step, nh)}, device_id_type=MESH
        )
        return 0

    lax.fori_loop(1, n, greet, 0)
    lax.fori_loop(1, nh, greet_head, 0)

    loads[0].wait()
    loads[1].wait()
    homes = home_ref[...]
    owners = lax.div(homes, jnp.full_like(homes, tok))
    docs = doc_ref[...].astype(F32)
    meta_ref[0:1, :] = owners.astype(F32)
    meta_ref[1:2, :] = (homes - owners * tok).astype(F32)
    meta_ref[2:3, :] = jnp.broadcast_to(docs[:, 0:1], (1, tok))
    meta_ref[3:4, :] = jnp.broadcast_to(docs[:, tok - 1 : tok], (1, tok))
    meta_ref[4:5, :] = docs
    meta_ref[5:8, :] = jnp.zeros((3, tok), F32)

    doc_row = jnp.broadcast_to(docs, (tok, tok))
    doc_col = doc_row.T
    first_doc, last_doc = meta_ref[2:3, :], meta_ref[3:4, :]
    place_row = lax.broadcasted_iota(jnp.int32, (tok, tok), 0)
    place_col = lax.broadcasted_iota(jnp.int32, (tok, tok), 1)
    visible = (doc_col == doc_row) & (place_col <= place_row)
    first_mask = doc_col == first_doc
    last_mask = doc_col == last_doc
    before = jnp.where(place_row < place_col, 1.0, 0.0).astype(BF16)
    metas[rows_at(me, 8), :] = meta_ref[...]

    def copy_meta(to, slot):
        return pltpu.make_async_remote_copy(
            src_ref=meta_ref, dst_ref=metas.at[rows_at(slot, 8)],
            send_sem=meta_sems.at[0, to], recv_sem=meta_sems.at[1, slot],
            device_id={"seq": to}, device_id_type=MESH,
        )

    def copy_rows(src, dst, sems, group, to, slot):
        return pltpu.make_async_remote_copy(
            src_ref=src.at[rows_at(group * n + to, cap)],
            dst_ref=dst.at[rows_at(group * n + slot, cap)],
            send_sem=sems.at[0, group, to], recv_sem=sems.at[1, group, slot],
            device_id={"seq": to}, device_id_type=MESH,
        )

    def others(body):
        def step(index, _):
            body(lax.rem(me + index, n))
            return 0

        lax.fori_loop(1, n, step, 0)

    def loop(count, body):
        def step(index, _):
            body(index)
            return 0

        lax.fori_loop(0, count, step, 0)

    def at_sub(block, part):
        return rows_from(block * quarter + part * sub, sub)

    def copy_near(sems, scan, src, dst, part, to, slot):
        return pltpu.make_async_remote_copy(
            src_ref=src.at[at_sub(to, part)], dst_ref=dst.at[at_sub(slot, part)],
            send_sem=sems.at[0, scan, to * SUBS + part],
            recv_sem=sems.at[1, scan, slot * SUBS + part],
            device_id={"seq": plane * PLANE + to}, device_id_type=MESH,
        )

    peers = [lax.rem(spot + step, PLANE) for step in range(1, PLANE)]

    def send_near(sems, scan, src, dst, part):
        for peer in peers:
            copy_near(sems, scan, src, dst, part, peer, spot).start()
        dst[at_sub(spot, part), :] = src[at_sub(spot, part), :]

    def got_near(sems, scan, src, dst, part):
        for peer in peers:
            copy_near(sems, scan, src, dst, part, peer, peer).wait_recv()

    def sent_near(sems, scan, src, dst, part):
        for peer in peers:
            copy_near(sems, scan, src, dst, part, peer, spot).wait_send()

    def copy_far(scan, total, far, part, ahead):
        sign = 1 if scan == 0 else -1
        return pltpu.make_async_remote_copy(
            src_ref=total.at[at_sub(0, part)], dst_ref=far.at[at_sub(ahead - 1, part)],
            send_sem=far_sems.at[0, scan, (ahead - 1) * SUBS + part],
            recv_sem=far_sems.at[1, scan, (ahead - 1) * SUBS + part],
            device_id={"seq": me + sign * ahead * PLANE}, device_id_type=MESH,
        )

    def sends(scan, ahead):
        return plane + ahead < planes if scan == 0 else plane >= ahead

    def gets(scan, ahead):
        return plane >= ahead if scan == 0 else plane + ahead < planes

    def doc(block, which):
        return metas[pl.ds(block * 8 + which, 1), :]

    scans = [
        (fw_own, fw_in, fw_total, fw_far, fw_send, fw_carry, 3, 2, list(range(PLANE)), -1),
        (rv_own, rv_in, rv_total, rv_far, rv_send, rv_carry, 2, 3, list(range(PLANE))[::-1], 1),
    ]
    for scan in range(2):
        far = scans[scan][3]
        for ahead in (1, 2):
            @pl.when(jnp.logical_not(gets(scan, ahead)))
            def _():
                far[(ahead - 1) * quarter : ahead * quarter, :] = jnp.zeros((quarter, HS), BF16)

    def plane_total(scan, part):
        own, arrived, total_ref, far, _, _, leaving, _, order, toward = scans[scan]
        got_near(near_sems, scan, own, arrived, part)
        total = None
        for block in order:
            mine = arrived[at_sub(block, part), :].astype(F32)
            here = plane * PLANE + block
            if total is None:
                total = mine
            else:
                total = mine + total * same(doc(here, leaving), doc(here + toward, leaving))
        total_ref[at_sub(0, part), :] = total.astype(BF16)
        for ahead in (1, 2):
            @pl.when(sends(scan, ahead))
            def _():
                copy_far(scan, total_ref, far, part, ahead).start()

    def carries(scan, part):
        _, arrived, total_ref, far, send, carry, leaving, entering, order, toward = scans[scan]
        for ahead in (1, 2):
            @pl.when(gets(scan, ahead))
            def _():
                copy_far(scan, total_ref, far, part, ahead).wait_recv()

        def clamp(block):
            return jnp.clip(block, 0, n - 1)

        edge = plane * PLANE + order[0] + toward
        total = far[at_sub(0, part), :].astype(F32) + far[at_sub(1, part), :].astype(F32) * same(
            doc(clamp(edge), leaving), doc(clamp(edge + toward * PLANE), leaving)
        )
        for block in order:
            here = plane * PLANE + block
            prior = doc(clamp(here + toward), leaving)
            send[at_sub(block, part), :] = (total * same(doc(here, entering), prior)).astype(BF16)
            mine = arrived[at_sub(block, part), :].astype(F32)
            total = mine + total * same(doc(here, leaving), prior)
        send_near(carry_sems, scan, send, carry, part)

    def got_carry(scan, part):
        got_near(carry_sems, scan, scans[scan][4], scans[scan][5], part)

    def group_heads(part):
        return [(index, index * SUBS + part) for index in range(each)]

    def own_forward(part):
        for _, head in group_heads(part):
            at = rows_at(head, HS)
            kept = jnp.where(last_mask, k_ref[:, at].astype(F32), 0.0).astype(BF16)
            fw_own[at, :] = dot(kept, v_ref[:, at], 0, 0).astype(BF16)

    def inside(part):
        for _, head in group_heads(part):
            at = rows_at(head, HS)
            attn = jnp.where(visible, dot(q_ref[:, at], k_ref[:, at], 1, 1), 0.0).astype(BF16)
            attn_ref[at, :] = attn
            o_ref[:, at] = dot(attn, v_ref[:, at], 1, 0)

    loads[2].wait()
    loads[3].wait()
    own_forward(0)
    pl.semaphore_wait(barrier, (n - 1) + (nh - 1))
    others(lambda other: copy_meta(other, me).start())
    if aligned:
        send_near(near_sems, 0, fw_own, fw_in, 0)

        def own_step(index):
            own_forward(index + 1)
            send_near(near_sems, 0, fw_own, fw_in, index + 1)

        loop(SUBS - 1, own_step)
    else:
        loop(SUBS - 1, lambda index: own_forward(index + 1))
        loop(SUBS, lambda part: send_near(near_sems, 0, fw_own, fw_in, part))
    loads[4].wait()
    loop(SUBS // 2, inside)
    others(lambda other: copy_meta(other, other).wait_recv())
    loop(SUBS, lambda part: plane_total(0, part))
    loop(SUBS // 2, lambda part: inside(part + SUBS // 2))

    slots = lax.broadcasted_iota(jnp.int32, (cap, tok), 0).astype(F32)
    lanes = lax.broadcasted_iota(jnp.int32, (cap, tok), 1).astype(F32)

    def picks(owners, owner):
        chosen = jnp.broadcast_to(jnp.where(owners == owner, 1.0, 0.0), (cap, tok))
        rank = dot(chosen.astype(BF16), before, 1, 0)
        return jnp.where(rank == slots, chosen, 0.0)

    def pack(owner):
        pack_ref[rows_at(owner, cap), :] = picks(meta_ref[0:1, :], owner.astype(F32)).astype(BF16)

    def unpack(source):
        chosen = picks(metas[pl.ds(source * 8, 1), :], me.astype(F32))
        row = jnp.sum(chosen * metas[pl.ds(source * 8 + 1, 1), :], axis=1, keepdims=True)
        used = jnp.sum(chosen, axis=1, keepdims=True)
        unpack_ref[rows_at(source, cap), :] = (
            jnp.where(row == lanes, 1.0, 0.0) * used
        ).astype(BF16)

    loop(SUBS, lambda part: carries(0, part))
    loop(n, pack)
    loads[5].wait()
    loads[6].wait()
    if not aligned:
        loop(SUBS, lambda part: got_carry(0, part))

    def output_step(part, sums):
        squares, inner = sums
        if aligned:
            got_carry(0, part)
        for _, head in group_heads(part):
            at = rows_at(head, HS)
            add = dot(q_ref[:, at], fw_carry[at, :], 1, 0)
            total = o_ref[:, at] + jnp.where(first_mask, add, 0.0)
            o_ref[:, at] = total
            scaled = gain_ref[:, at] * gn_ref[:, at].astype(F32)
            squares, inner = squares + total * total, inner + scaled * total
        return squares, inner

    zero = jnp.zeros((tok, HS), F32)
    squares, inner = lax.fori_loop(0, SUBS, output_step, (zero, zero))
    squares = jnp.sum(squares, axis=1, keepdims=True)
    inner = jnp.sum(inner, axis=1, keepdims=True)
    pair = jnp.where(place_col < HS // 2, squares, inner)
    sums_out[...] = pair

    def sum_copy(to, slot):
        return pltpu.make_async_remote_copy(
            src_ref=sums_out, dst_ref=sums_in.at[rows_at(slot, tok)],
            send_sem=sum_sems.at[0, to], recv_sem=sum_sems.at[1, slot],
            device_id={"head": to}, device_id_type=MESH,
        )

    def sum_start(step, _):
        sum_copy(lax.rem(me_head + step, nh), me_head).start()
        return 0

    def sum_finish(step, total):
        other = lax.rem(me_head + step, nh)
        sum_copy(other, other).wait_recv()
        return total + sums_in[rows_at(other, tok), :]

    def sum_sent(step, _):
        sum_copy(lax.rem(me_head + step, nh), me_head).wait_send()
        return 0

    lax.fori_loop(1, nh, sum_start, 0)
    loop(n, unpack)
    pair = lax.fori_loop(1, nh, sum_finish, pair)
    full = HEADS * HS
    inv_rms = lax.rsqrt(pair[:, 0:1] / full + EPSILON)
    pull = inv_rms * inv_rms * inv_rms * pair[:, HS - 1 : HS] / full
    inv_rms = jnp.broadcast_to(inv_rms, (tok, HS))
    pull = jnp.broadcast_to(pull, (tok, HS))

    def own_reverse(part):
        for _, head in group_heads(part):
            at = rows_at(head, HS)
            scaled = gain_ref[:, at] * gn_ref[:, at].astype(F32)
            grad = (inv_rms * scaled - o_ref[:, at] * pull).astype(BF16)
            go_ref[:, at] = grad
            kept = jnp.where(first_mask, q_ref[:, at].astype(F32), 0.0).astype(BF16)
            rv_own[at, :] = dot(kept, grad, 0, 0).astype(BF16)
        if aligned:
            send_near(near_sems, 1, rv_own, rv_in, part)

    loop(SUBS, own_reverse)
    if not aligned:
        loop(SUBS, lambda part: send_near(near_sems, 1, rv_own, rv_in, part))

    half = SUBS // 2
    slots_all = n * cap

    def grad_query(group, part):
        for index, head in group_heads(group * half + part):
            at = rows_at(head, HS)
            grad = go_ref[:, at]
            back = jnp.where(visible, dot(grad, v_ref[:, at], 1, 1), 0.0).astype(BF16)
            back_ref[at, :] = back
            add = dot(grad, fw_carry[at, :], 1, 1)
            result = dot(back, k_ref[:, at], 1, 0) + jnp.where(first_mask, add, 0.0)
            bq_send[
                group * slots_all : (group + 1) * slots_all, rows_at(part * each + index, HS)
            ] = dot(pack_ref[...], result.astype(BF16), 1, 0).astype(BF16)

    def send_query(group):
        others(lambda other: copy_rows(bq_send, bq_in, q_sems, group, other, me).start())
        bq_in[rows_at(group * n + me, cap), :] = bq_send[rows_at(group * n + me, cap), :]

    loop(half, lambda part: grad_query(0, part))
    loop(SUBS, lambda part: plane_total(1, part))
    send_query(0)
    loop(half, lambda part: grad_query(1, part))
    send_query(1)

    def inside_back(part):
        for _, head in group_heads(part):
            at = rows_at(head, HS)
            gk_ref[:, at] = dot(back_ref[at, :], q_ref[:, at], 0, 0)
            gv_ref[:, at] = dot(attn_ref[at, :], go_ref[:, at], 0, 0)

    loop(SUBS, lambda part: carries(1, part))
    loop(SUBS, inside_back)
    if not aligned:
        loop(SUBS, lambda part: got_carry(1, part))

    def grad_pair(part):
        if aligned:
            got_carry(1, part)
        rows = rows_at(part, slots_all)
        for index, head in group_heads(part):
            at = rows_at(head, HS)
            carry = rv_carry[at, :]
            key = gk_ref[:, at] + jnp.where(last_mask, dot(v_ref[:, at], carry, 1, 1), 0.0)
            value = gv_ref[:, at] + jnp.where(last_mask, dot(k_ref[:, at], carry, 1, 0), 0.0)
            for which, result in enumerate((key, value)):
                column = (which * each + index) * HS
                bkv_send[rows, column : column + HS] = dot(
                    pack_ref[...], result.astype(BF16), 1, 0
                ).astype(BF16)
        others(lambda other: copy_rows(bkv_send, bkv_in, kv_sems, part, other, me).start())
        bkv_in[rows_at(part * n + me, cap), :] = bkv_send[rows_at(part * n + me, cap), :]

    loop(SUBS, grad_pair)

    def place_query(group, part):
        for index, head in group_heads(group * half + part):
            arrived = bq_in[
                group * slots_all : (group + 1) * slots_all, rows_at(part * each + index, HS)
            ]
            out_ref[:, rows_at(head, HS)] = dot(unpack_ref[...], arrived, 0, 0).astype(BF16)

    for group in range(2):
        others(lambda other: copy_rows(bq_send, bq_in, q_sems, group, other, other).wait_recv())
        loop(half, lambda part: place_query(group, part))

    def place_pair(part):
        others(lambda other: copy_rows(bkv_send, bkv_in, kv_sems, part, other, other).wait_recv())
        rows = rows_at(part, slots_all)
        for index, head in group_heads(part):
            for which in range(2):
                column = (which * each + index) * HS
                out_ref[:, rows_at((which + 1) * heads + head, HS)] = dot(
                    unpack_ref[...], bkv_in[rows, column : column + HS], 0, 0
                ).astype(BF16)

    loop(SUBS, place_pair)

    others(lambda other: copy_meta(other, me).wait_send())
    lax.fori_loop(1, nh, sum_sent, 0)
    for scan in range(2):
        own, arrived, total_ref, far, send, carry = scans[scan][:6]

        def drain(part):
            sent_near(near_sems, scan, own, arrived, part)
            sent_near(carry_sems, scan, send, carry, part)
            for ahead in (1, 2):
                @pl.when(sends(scan, ahead))
                def _():
                    copy_far(scan, total_ref, far, part, ahead).wait_send()

        loop(SUBS, drain)
    for group in range(2):
        others(lambda other: copy_rows(bq_send, bq_in, q_sems, group, other, me).wait_send())
    loop(
        SUBS,
        lambda part: others(
            lambda other: copy_rows(bkv_send, bkv_in, kv_sems, part, other, me).wait_send()
        ),
    )


def local(n, nh, query, keys, values, grad_normed, norm_gain, doc_ids, home):
    tok, width = query.shape
    heads = width // HS
    cap = max(16, 2 * tok // n)
    states = pltpu.VMEM((heads * HS, HS), BF16)
    total = pltpu.VMEM((heads * HS // PLANE, HS), BF16)
    far = pltpu.VMEM((2 * heads * HS // PLANE, HS), BF16)
    scan = [states, states, total, far, states, states]
    block = pltpu.VMEM((tok, width), BF16)
    wide = pltpu.VMEM((tok, width), F32)
    map_rows = pltpu.VMEM((n * cap, tok), BF16)
    query_rows = pltpu.VMEM((2 * n * cap, width // 2), BF16)
    pair_rows = pltpu.VMEM((SUBS * n * cap, 2 * width // SUBS), BF16)
    dma = pltpu.SemaphoreType.DMA
    result = pl.pallas_call(
        functools.partial(kernel, n, nh, cap),
        out_shape=jax.ShapeDtypeStruct((tok, 3 * width), BF16),
        in_specs=[pl.BlockSpec(memory_space=pl.ANY)] * 7,
        out_specs=pl.BlockSpec(memory_space=pltpu.VMEM),
        scratch_shapes=[
            block, block, block, block,
            pltpu.VMEM((1, width), F32),
            pltpu.VMEM((1, tok), jnp.int32),
            pltpu.VMEM((1, tok), jnp.int32),
            pltpu.VMEM((8, tok), F32),
            pltpu.VMEM((n * 8, tok), F32),
            *scan, *scan,
            states, states,
            wide, block, wide, wide,
            pltpu.VMEM((tok, HS), F32),
            pltpu.VMEM((nh * tok, HS), F32),
            map_rows, map_rows,
            query_rows, query_rows, pair_rows, pair_rows,
            dma((7,)),
            dma((2, n)),
            dma((2, 2, PLANE * SUBS)),
            dma((2, 2, 2 * SUBS)),
            dma((2, 2, PLANE * SUBS)),
            dma((2, 2, n)),
            dma((2, SUBS, n)),
            dma((2, nh)),
        ],
        compiler_params=pltpu.CompilerParams(
            collective_id=0, has_side_effects=True, vmem_limit_bytes=48 * 1024 * 1024
        ),
    )(query, keys, values, grad_normed, norm_gain[None, :], doc_ids[None, :], home[None, :])
    return result.reshape(tok, 3, width)


def solution(mesh):
    placed = (
        P("seq", "head"),
        P("seq", "head"),
        P("seq", "head"),
        P("seq", "head"),
        P("head"),
        P("seq"),
        P("seq"),
    )
    return jax.shard_map(
        functools.partial(local, mesh.shape["seq"], mesh.shape["head"]),
        mesh=mesh, in_specs=placed, out_specs=P("seq", None, "head"), check_vma=False,
    )
```

time: 153 us -> 120 us (0.78)
  the two profiles are of different devices: /device:TPU:31 before, /device:TPU:0 now
where the time goes in v2:
time: 120 us
  Pallas kernels  111 us (92%)
  local copies, waits for them, and re-layouts  8.64 us (7%)
    pallas_call x1, Pallas kernels, local(): pl.pallas_call(functools.partial(kernel, n, nh, cap), out_shape=jax.Shape...  111 us
    unnamed x14, local copies, waits for them, and re-layouts  6.17 us

profile of v2, /device:TPU:0, one launch (start us, length us, event | category | flops | bytes accessed | tf_op | source)
XLA Modules:
  0.0 119.6 jit_solution(9788310648264794840)
XLA Ops:
  0.0 0.0 copy-start
  0.0 1.0 copy-done
  1.0 0.0 copy-start.1
  1.0 1.0 copy-done.1
  2.1 0.0 copy-start.2
  2.1 1.0 copy-done.2
  3.1 0.0 copy-start.3
  3.1 1.0 copy-done.3
  4.2 0.0 copy-start.4
  4.2 0.7 copy-done.4
  4.9 0.0 copy-start.5
  4.9 0.7 copy-done.5
  5.5 0.0 copy-start.6
  5.5 0.7 copy-done.6
  6.2 110.9 %shard_map.73 = bf16[128,6144]{1,0:T(8,128)(2,1)S(1)} custom-call(bf16[128,2048]{1,0:T(8,128)(2,1)S(1)} %copy-done, bf16[128,2048]{1,0:T(8,128)(2,1)S(1)} %copy-done.1, bf16[128,2048]{1,0:T(8,128)(2,1)S(1)} %copy-done.2, bf16[128,2048]{1,0:T(8,128)(2,1)S(1)} %copy-done.3, f32[1,2048]{1,0:T(1,128)S(1)} %bitcast.4, s32[1,128]{1,0:T(1,128)S(1)} %bitcast.5, ...), custom_call_target="tpu_custom_call" | custom-call | tf_op jit(solution)/shard_map/pallas_call | solution.py:485
  117.1 0.9 copy.9
  118.0 1.6 %copy.10 = bf16[128,3,2048]{2,0,1:T(8,128)(2,1)} copy(bf16[128,3,2048]{0,2,1:T(8,128)(2,1)S(1)} %bitcast.7) | data formatting | bytes 3145728 | tf_op jit(solution)/shard_map/reshape | solution.py:517
Async XLA Ops:
  0.0 1.0 copy-start
  1.0 1.0 copy-start.1
  2.1 1.0 copy-start.2
  3.1 1.0 copy-start.3
  4.2 0.7 copy-start.4
  4.9 0.7 copy-start.5
  5.5 0.7 copy-start.6

commit v3 on v2

--- a/solution.py
+++ b/solution.py
@@ -129,10 +129,11 @@
 
     def others(body):
         def step(index, _):
-            body(lax.rem(me + index, n))
+            away = (index + 1) // 2
+            body(lax.rem(me + n // 2 + away * (1 - 2 * lax.rem(index, 2)), n))
             return 0
 
-        lax.fori_loop(1, n, step, 0)
+        lax.fori_loop(0, n - 1, step, 0)
 
     def loop(count, body):
         def step(index, _):
@@ -195,6 +196,29 @@
             @pl.when(jnp.logical_not(gets(scan, ahead)))
             def _():
                 far[(ahead - 1) * quarter : ahead * quarter, :] = jnp.zeros((quarter, HS), BF16)
+
+    def chain(scan, part):
+        own, arrived, total_ref, far, send, carry, leaving, entering, order, toward = scans[scan]
+        got_near(near_sems, scan, own, arrived, part)
+
+        @pl.when(gets(scan, 1))
+        def _():
+            copy_far(scan, total_ref, far, part, 1).wait_recv()
+
+        total = far[at_sub(0, part), :].astype(F32)
+        for block in order:
+            here = plane * PLANE + block
+            prior = doc(jnp.clip(here + toward, 0, n - 1), leaving)
+            send[at_sub(block, part), :] = (total * same(doc(here, entering), prior)).astype(BF16)
+            mine = arrived[at_sub(block, part), :].astype(F32)
+            total = mine + total * same(doc(here, leaving), prior)
+        total_ref[at_sub(0, part), :] = total.astype(BF16)
+
+        @pl.when(sends(scan, 1))
+        def _():
+            copy_far(scan, total_ref, far, part, 1).start()
+
+        send_near(carry_sems, scan, send, carry, part)
 
     def plane_total(scan, part):
         own, arrived, total_ref, far, _, _, leaving, _, order, toward = scans[scan]
@@ -273,7 +297,7 @@
     loads[4].wait()
     loop(SUBS // 2, inside)
     others(lambda other: copy_meta(other, other).wait_recv())
-    loop(SUBS, lambda part: plane_total(0, part))
+    loop(SUBS, lambda part: chain(0, part))
     loop(SUBS // 2, lambda part: inside(part + SUBS // 2))
 
     slots = lax.broadcasted_iota(jnp.int32, (cap, tok), 0).astype(F32)
@@ -295,7 +319,6 @@
             jnp.where(row == lanes, 1.0, 0.0) * used
         ).astype(BF16)
 
-    loop(SUBS, lambda part: carries(0, part))
     loop(n, pack)
     loads[5].wait()
     loads[6].wait()
@@ -426,7 +449,7 @@
             arrived = bq_in[
                 group * slots_all : (group + 1) * slots_all, rows_at(part * each + index, HS)
             ]
-            out_ref[:, rows_at(head, HS)] = dot(unpack_ref[...], arrived, 0, 0).astype(BF16)
+            out_ref[0, :, rows_at(head, HS)] = dot(unpack_ref[...], arrived, 0, 0).astype(BF16)
 
     for group in range(2):
         others(lambda other: copy_rows(bq_send, bq_in, q_sems, group, other, other).wait_recv())
@@ -438,7 +461,7 @@
         for index, head in group_heads(part):
             for which in range(2):
                 column = (which * each + index) * HS
-                out_ref[:, rows_at((which + 1) * heads + head, HS)] = dot(
+                out_ref[which + 1, :, rows_at(head, HS)] = dot(
                     unpack_ref[...], bkv_in[rows, column : column + HS], 0, 0
                 ).astype(BF16)
 
@@ -452,7 +475,7 @@
         def drain(part):
             sent_near(near_sems, scan, own, arrived, part)
             sent_near(carry_sems, scan, send, carry, part)
-            for ahead in (1, 2):
+            for ahead in (1, 2)[: scan + 1]:
                 @pl.when(sends(scan, ahead))
                 def _():
                     copy_far(scan, total_ref, far, part, ahead).wait_send()
@@ -484,8 +507,8 @@
     dma = pltpu.SemaphoreType.DMA
     result = pl.pallas_call(
         functools.partial(kernel, n, nh, cap),
-        out_shape=jax.ShapeDtypeStruct((tok, 3 * width), BF16),
-        in_specs=[pl.BlockSpec(memory_space=pl.ANY)] * 7,
+        out_shape=jax.ShapeDtypeStruct((3, tok, width), BF16),
+        in_specs=[pl.BlockSpec(memory_space=pltpu.HBM)] * 7,
         out_specs=pl.BlockSpec(memory_space=pltpu.VMEM),
         scratch_shapes=[
             block, block, block, block,
@@ -511,10 +534,10 @@
             dma((2, nh)),
         ],
         compiler_params=pltpu.CompilerParams(
-            collective_id=0, has_side_effects=True, vmem_limit_bytes=48 * 1024 * 1024
+            collective_id=0, has_side_effects=True, vmem_limit_bytes=56 * 1024 * 1024
         ),
     )(query, keys, values, grad_normed, norm_gain[None, :], doc_ids[None, :], home[None, :])
-    return result.reshape(tok, 3, width)
+    return jnp.transpose(result, (1, 0, 2))
 
 
 def solution(mesh):

time: 120 us -> 120 us (level)
  Pallas kernels: 111 us -> 117 us
  local copies, waits for them, and re-layouts: 8.64 us -> 2.73 us
    pallas_call x1, Pallas kernels: 111 us -> 117 us  [local(): pl.pallas_call(functools.partial(kernel, n, nh, cap), out_shape=jax.Shape...]
    unnamed x14 -> x1, local copies, waits for them, and re-layouts: 6.17 us -> 2.73 us
    reshape x1 -> x0, local copies, waits for them, and re-layouts: 1.57 us -> none  [local(): return result.reshape(tok, 3, width)]
where the time goes in v3:
time: 120 us; the launch traced here: 119 us
  Pallas kernels  117 us (98%)
  local copies, waits for them, and re-layouts  2.73 us (2%)
    pallas_call x1, Pallas kernels, local(): pl.pallas_call(functools.partial(kernel, n, nh, cap), out_shape=jax.Shape...  117 us
    unnamed x1, local copies, waits for them, and re-layouts  2.73 us

profile of v3, /device:TPU:0, one launch (start us, length us, event | category | flops | bytes accessed | tf_op | source)
XLA Modules:
  0.0 119.4 jit_solution(17813175911768697611)
XLA Ops:
  0.0 116.7 %shard_map.73 = bf16[3,128,2048]{2,1,0:T(8,128)(2,1)} custom-call(bf16[128,2048]{1,0:T(8,128)(2,1)} %q_hbm.1, bf16[128,2048]{1,0:T(8,128)(2,1)} %k_hbm.1, bf16[128,2048]{1,0:T(8,128)(2,1)} %v_hbm.1, bf16[128,2048]{1,0:T(8,128)(2,1)} %gn_hbm.1, f32[1,2048]{1,0:T(1,128)} %bitcast.5, s32[1,128]{1,0:T(1,128)} %bitcast.6, s32[1,128]{1,0:T(1,128)} %bitcast.7), custom_call_target="tpu_custom_call" | custom-call | tf_op jit(solution)/shard_map/pallas_call | solution.py:508
  116.7 2.7 %copy.9 = bf16[128,3,2048]{2,0,1:T(8,128)(2,1)} copy(bf16[128,3,2048]{2,0,1:T(8,128)(2,1)} %bitcast.4) | data formatting | bytes 3145728

commit v4 on v3

--- a/solution.py
+++ b/solution.py
@@ -46,7 +46,7 @@
     fw_own, fw_in, fw_total, fw_far, fw_send, fw_carry,
     rv_own, rv_in, rv_total, rv_far, rv_send, rv_carry,
     attn_ref, back_ref, o_ref, go_ref, gk_ref, gv_ref, sums_out, sums_in,
-    pack_ref, unpack_ref, bq_send, bq_in, bkv_send, bkv_in,
+    rank_ref, pack_ref, unpack_ref, place_ref, bq_send, bq_in, bkv_send, bkv_in,
     in_sem, meta_sems, near_sems, far_sems, carry_sems, q_sems, kv_sems, sum_sems,
 ):
     tok, width = q_ref.shape
@@ -129,11 +129,10 @@
 
     def others(body):
         def step(index, _):
-            away = (index + 1) // 2
-            body(lax.rem(me + n // 2 + away * (1 - 2 * lax.rem(index, 2)), n))
+            body(lax.rem(me + index, n))
             return 0
 
-        lax.fori_loop(0, n - 1, step, 0)
+        lax.fori_loop(1, n, step, 0)
 
     def loop(count, body):
         def step(index, _):
@@ -282,7 +281,6 @@
     loads[3].wait()
     own_forward(0)
     pl.semaphore_wait(barrier, (n - 1) + (nh - 1))
-    others(lambda other: copy_meta(other, me).start())
     if aligned:
         send_near(near_sems, 0, fw_own, fw_in, 0)
 
@@ -294,12 +292,7 @@
     else:
         loop(SUBS - 1, lambda index: own_forward(index + 1))
         loop(SUBS, lambda part: send_near(near_sems, 0, fw_own, fw_in, part))
-    loads[4].wait()
-    loop(SUBS // 2, inside)
-    others(lambda other: copy_meta(other, other).wait_recv())
-    loop(SUBS, lambda part: chain(0, part))
-    loop(SUBS // 2, lambda part: inside(part + SUBS // 2))
-
+    others(lambda other: copy_meta(other, me).start())
     slots = lax.broadcasted_iota(jnp.int32, (cap, tok), 0).astype(F32)
     lanes = lax.broadcasted_iota(jnp.int32, (cap, tok), 1).astype(F32)
 
@@ -308,8 +301,21 @@
         rank = dot(chosen.astype(BF16), before, 1, 0)
         return jnp.where(rank == slots, chosen, 0.0)
 
+    owner_row = meta_ref[0:1, :]
+    owner_of = lax.broadcasted_iota(jnp.int32, (n, tok), 0).astype(F32)
+    rank_ref[...] = dot(same(owner_row, owner_of).astype(BF16), before, 1, 0)
+
     def pack(owner):
-        pack_ref[rows_at(owner, cap), :] = picks(meta_ref[0:1, :], owner.astype(F32)).astype(BF16)
+        rank = rank_ref[pl.ds(owner, 1), :]
+        chosen = same(owner_row, owner.astype(F32))
+        pack_ref[rows_at(owner, cap), :] = (same(rank, slots) * chosen).astype(BF16)
+
+    loads[4].wait()
+    loop(SUBS // 2, inside)
+    loop(n, pack)
+    others(lambda other: copy_meta(other, other).wait_recv())
+    loop(SUBS, lambda part: chain(0, part))
+    loop(SUBS // 2, lambda part: inside(part + SUBS // 2))
 
     def unpack(source):
         chosen = picks(metas[pl.ds(source * 8, 1), :], me.astype(F32))
@@ -319,7 +325,6 @@
             jnp.where(row == lanes, 1.0, 0.0) * used
         ).astype(BF16)
 
-    loop(n, pack)
     loads[5].wait()
     loads[6].wait()
     if not aligned:
@@ -366,7 +371,6 @@
         return 0
 
     lax.fori_loop(1, nh, sum_start, 0)
-    loop(n, unpack)
     pair = lax.fori_loop(1, nh, sum_finish, pair)
     full = HEADS * HS
     inv_rms = lax.rsqrt(pair[:, 0:1] / full + EPSILON)
@@ -393,6 +397,7 @@
     slots_all = n * cap
 
     def grad_query(group, part):
+        made = []
         for index, head in group_heads(group * half + part):
             at = rows_at(head, HS)
             grad = go_ref[:, at]
@@ -400,9 +405,10 @@
             back_ref[at, :] = back
             add = dot(grad, fw_carry[at, :], 1, 1)
             result = dot(back, k_ref[:, at], 1, 0) + jnp.where(first_mask, add, 0.0)
-            bq_send[
-                group * slots_all : (group + 1) * slots_all, rows_at(part * each + index, HS)
-            ] = dot(pack_ref[...], result.astype(BF16), 1, 0).astype(BF16)
+            made.append(result.astype(BF16))
+        bq_send[group * slots_all : (group + 1) * slots_all, rows_at(part, each * HS)] = dot(
+            pack_ref[...], jnp.concatenate(made, axis=1), 1, 0
+        ).astype(BF16)
 
     def send_query(group):
         others(lambda other: copy_rows(bq_send, bq_in, q_sems, group, other, me).start())
@@ -428,28 +434,30 @@
     def grad_pair(part):
         if aligned:
             got_carry(1, part)
-        rows = rows_at(part, slots_all)
+        made = [[], []]
         for index, head in group_heads(part):
             at = rows_at(head, HS)
             carry = rv_carry[at, :]
             key = gk_ref[:, at] + jnp.where(last_mask, dot(v_ref[:, at], carry, 1, 1), 0.0)
             value = gv_ref[:, at] + jnp.where(last_mask, dot(k_ref[:, at], carry, 1, 0), 0.0)
-            for which, result in enumerate((key, value)):
-                column = (which * each + index) * HS
-                bkv_send[rows, column : column + HS] = dot(
-                    pack_ref[...], result.astype(BF16), 1, 0
-                ).astype(BF16)
+            made[0].append(key.astype(BF16))
+            made[1].append(value.astype(BF16))
+        bkv_send[rows_at(part, slots_all), :] = dot(
+            pack_ref[...], jnp.concatenate(made[0] + made[1], axis=1), 1, 0
+        ).astype(BF16)
         others(lambda other: copy_rows(bkv_send, bkv_in, kv_sems, part, other, me).start())
         bkv_in[rows_at(part * n + me, cap), :] = bkv_send[rows_at(part * n + me, cap), :]
 
     loop(SUBS, grad_pair)
 
+    loop(n, unpack)
+    place_ref[...] = unpack_ref[...].T
+
     def place_query(group, part):
+        arrived = bq_in[group * slots_all : (group + 1) * slots_all, rows_at(part, each * HS)]
+        placed = dot(place_ref[...], arrived, 1, 0).astype(BF16)
         for index, head in group_heads(group * half + part):
-            arrived = bq_in[
-                group * slots_all : (group + 1) * slots_all, rows_at(part * each + index, HS)
-            ]
-            out_ref[0, :, rows_at(head, HS)] = dot(unpack_ref[...], arrived, 0, 0).astype(BF16)
+            out_ref[0, :, rows_at(head, HS)] = placed[:, index * HS : (index + 1) * HS]
 
     for group in range(2):
         others(lambda other: copy_rows(bq_send, bq_in, q_sems, group, other, other).wait_recv())
@@ -457,13 +465,11 @@
 
     def place_pair(part):
         others(lambda other: copy_rows(bkv_send, bkv_in, kv_sems, part, other, other).wait_recv())
-        rows = rows_at(part, slots_all)
+        placed = dot(place_ref[...], bkv_in[rows_at(part, slots_all), :], 1, 0).astype(BF16)
         for index, head in group_heads(part):
             for which in range(2):
                 column = (which * each + index) * HS
-                out_ref[which + 1, :, rows_at(head, HS)] = dot(
-                    unpack_ref[...], bkv_in[rows, column : column + HS], 0, 0
-                ).astype(BF16)
+                out_ref[which + 1, :, rows_at(head, HS)] = placed[:, column : column + HS]
 
     loop(SUBS, place_pair)
 
@@ -522,7 +528,9 @@
             wide, block, wide, wide,
             pltpu.VMEM((tok, HS), F32),
             pltpu.VMEM((nh * tok, HS), F32),
+            pltpu.VMEM((n, tok), F32),
             map_rows, map_rows,
+            pltpu.VMEM((tok, n * cap), BF16),
             query_rows, query_rows, pair_rows, pair_rows,
             dma((7,)),
             dma((2, n)),

time: 120 us -> 117 us (0.975)
  Pallas kernels: 117 us -> 113 us
    pallas_call x1, Pallas kernels: 117 us -> 113 us  [local(): pl.pallas_call(functools.partial(kernel, n, nh, cap), out_shape=jax.Shape...]
where the time goes in v4:
time: 117 us; the launch traced here: 115 us
  Pallas kernels  113 us (97%)
  local copies, waits for them, and re-layouts  2.73 us (2%)
    pallas_call x1, Pallas kernels, local(): pl.pallas_call(functools.partial(kernel, n, nh, cap), out_shape=jax.Shape...  113 us
    unnamed x1, local copies, waits for them, and re-layouts  2.73 us

profile of v4, /device:TPU:0, one launch (start us, length us, event | category | flops | bytes accessed | tf_op | source)
XLA Modules:
  0.0 115.3 jit_solution(2905648283963128745)
XLA Ops:
  0.0 112.6 %shard_map.73 = bf16[3,128,2048]{2,1,0:T(8,128)(2,1)} custom-call(bf16[128,2048]{1,0:T(8,128)(2,1)} %q_hbm.1, bf16[128,2048]{1,0:T(8,128)(2,1)} %k_hbm.1, bf16[128,2048]{1,0:T(8,128)(2,1)} %v_hbm.1, bf16[128,2048]{1,0:T(8,128)(2,1)} %gn_hbm.1, f32[1,2048]{1,0:T(1,128)} %bitcast.5, s32[1,128]{1,0:T(1,128)} %bitcast.6, s32[1,128]{1,0:T(1,128)} %bitcast.7), custom_call_target="tpu_custom_call" | custom-call | tf_op jit(solution)/shard_map/pallas_call | solution.py:514
  112.6 2.7 %copy.9 = bf16[128,3,2048]{2,0,1:T(8,128)(2,1)} copy(bf16[128,3,2048]{2,0,1:T(8,128)(2,1)} %bitcast.4) | data formatting | bytes 3145728

commit v5 on v4

--- a/solution.py
+++ b/solution.py
@@ -167,20 +167,19 @@
         for peer in peers:
             copy_near(sems, scan, src, dst, part, peer, spot).wait_send()
 
-    def copy_far(scan, total, far, part, ahead):
+    def copy_far(scan, total, far, part):
         sign = 1 if scan == 0 else -1
         return pltpu.make_async_remote_copy(
-            src_ref=total.at[at_sub(0, part)], dst_ref=far.at[at_sub(ahead - 1, part)],
-            send_sem=far_sems.at[0, scan, (ahead - 1) * SUBS + part],
-            recv_sem=far_sems.at[1, scan, (ahead - 1) * SUBS + part],
-            device_id={"seq": me + sign * ahead * PLANE}, device_id_type=MESH,
-        )
-
-    def sends(scan, ahead):
-        return plane + ahead < planes if scan == 0 else plane >= ahead
-
-    def gets(scan, ahead):
-        return plane >= ahead if scan == 0 else plane + ahead < planes
+            src_ref=total.at[at_sub(0, part)], dst_ref=far.at[at_sub(0, part)],
+            send_sem=far_sems.at[0, scan, part], recv_sem=far_sems.at[1, scan, part],
+            device_id={"seq": me + sign * PLANE}, device_id_type=MESH,
+        )
+
+    def sends(scan):
+        return plane + 1 < planes if scan == 0 else plane >= 1
+
+    def gets(scan):
+        return plane >= 1 if scan == 0 else plane + 1 < planes
 
     def doc(block, which):
         return metas[pl.ds(block * 8 + which, 1), :]
@@ -191,18 +190,18 @@
     ]
     for scan in range(2):
         far = scans[scan][3]
-        for ahead in (1, 2):
-            @pl.when(jnp.logical_not(gets(scan, ahead)))
-            def _():
-                far[(ahead - 1) * quarter : ahead * quarter, :] = jnp.zeros((quarter, HS), BF16)
+
+        @pl.when(jnp.logical_not(gets(scan)))
+        def _():
+            far[...] = jnp.zeros((quarter, HS), BF16)
 
     def chain(scan, part):
         own, arrived, total_ref, far, send, carry, leaving, entering, order, toward = scans[scan]
         got_near(near_sems, scan, own, arrived, part)
 
-        @pl.when(gets(scan, 1))
+        @pl.when(gets(scan))
         def _():
-            copy_far(scan, total_ref, far, part, 1).wait_recv()
+            copy_far(scan, total_ref, far, part).wait_recv()
 
         total = far[at_sub(0, part), :].astype(F32)
         for block in order:
@@ -213,49 +212,10 @@
             total = mine + total * same(doc(here, leaving), prior)
         total_ref[at_sub(0, part), :] = total.astype(BF16)
 
-        @pl.when(sends(scan, 1))
+        @pl.when(sends(scan))
         def _():
-            copy_far(scan, total_ref, far, part, 1).start()
-
-        send_near(carry_sems, scan, send, carry, part)
-
-    def plane_total(scan, part):
-        own, arrived, total_ref, far, _, _, leaving, _, order, toward = scans[scan]
-        got_near(near_sems, scan, own, arrived, part)
-        total = None
-        for block in order:
-            mine = arrived[at_sub(block, part), :].astype(F32)
-            here = plane * PLANE + block
-            if total is None:
-                total = mine
-            else:
-                total = mine + total * same(doc(here, leaving), doc(here + toward, leaving))
-        total_ref[at_sub(0, part), :] = total.astype(BF16)
-        for ahead in (1, 2):
-            @pl.when(sends(scan, ahead))
-            def _():
-                copy_far(scan, total_ref, far, part, ahead).start()
-
-    def carries(scan, part):
-        _, arrived, total_ref, far, send, carry, leaving, entering, order, toward = scans[scan]
-        for ahead in (1, 2):
-            @pl.when(gets(scan, ahead))
-            def _():
-                copy_far(scan, total_ref, far, part, ahead).wait_recv()
-
-        def clamp(block):
-            return jnp.clip(block, 0, n - 1)
-
-        edge = plane * PLANE + order[0] + toward
-        total = far[at_sub(0, part), :].astype(F32) + far[at_sub(1, part), :].astype(F32) * same(
-            doc(clamp(edge), leaving), doc(clamp(edge + toward * PLANE), leaving)
-        )
-        for block in order:
-            here = plane * PLANE + block
-            prior = doc(clamp(here + toward), leaving)
-            send[at_sub(block, part), :] = (total * same(doc(here, entering), prior)).astype(BF16)
-            mine = arrived[at_sub(block, part), :].astype(F32)
-            total = mine + total * same(doc(here, leaving), prior)
+            copy_far(scan, total_ref, far, part).start()
+
         send_near(carry_sems, scan, send, carry, part)
 
     def got_carry(scan, part):
@@ -414,11 +374,11 @@
         others(lambda other: copy_rows(bq_send, bq_in, q_sems, group, other, me).start())
         bq_in[rows_at(group * n + me, cap), :] = bq_send[rows_at(group * n + me, cap), :]
 
-    loop(half, lambda part: grad_query(0, part))
-    loop(SUBS, lambda part: plane_total(1, part))
-    send_query(0)
-    loop(half, lambda part: grad_query(1, part))
-    send_query(1)
+    for group in range(2):
+        loop(half, lambda part: grad_query(group, part))
+    loop(SUBS, lambda part: chain(1, part))
+    for group in range(2):
+        send_query(group)
 
     def inside_back(part):
         for _, head in group_heads(part):
@@ -426,7 +386,6 @@
             gk_ref[:, at] = dot(back_ref[at, :], q_ref[:, at], 0, 0)
             gv_ref[:, at] = dot(attn_ref[at, :], go_ref[:, at], 0, 0)
 
-    loop(SUBS, lambda part: carries(1, part))
     loop(SUBS, inside_back)
     if not aligned:
         loop(SUBS, lambda part: got_carry(1, part))
@@ -481,10 +440,10 @@
         def drain(part):
             sent_near(near_sems, scan, own, arrived, part)
             sent_near(carry_sems, scan, send, carry, part)
-            for ahead in (1, 2)[: scan + 1]:
-                @pl.when(sends(scan, ahead))
-                def _():
-                    copy_far(scan, total_ref, far, part, ahead).wait_send()
+
+            @pl.when(sends(scan))
+            def _():
+                copy_far(scan, total_ref, far, part).wait_send()
 
         loop(SUBS, drain)
     for group in range(2):
@@ -503,7 +462,7 @@
     cap = max(16, 2 * tok // n)
     states = pltpu.VMEM((heads * HS, HS), BF16)
     total = pltpu.VMEM((heads * HS // PLANE, HS), BF16)
-    far = pltpu.VMEM((2 * heads * HS // PLANE, HS), BF16)
+    far = pltpu.VMEM((heads * HS // PLANE, HS), BF16)
     scan = [states, states, total, far, states, states]
     block = pltpu.VMEM((tok, width), BF16)
     wide = pltpu.VMEM((tok, width), F32)
@@ -535,7 +494,7 @@
             dma((7,)),
             dma((2, n)),
             dma((2, 2, PLANE * SUBS)),
-            dma((2, 2, 2 * SUBS)),
+            dma((2, 2, SUBS)),
             dma((2, 2, PLANE * SUBS)),
             dma((2, 2, n)),
             dma((2, SUBS, n)),

time: 117 us -> 125 us (1.068)
  the two profiles are of different devices: /device:TPU:0 before, /device:TPU:28 now
where the time goes in v5:
time: 125 us
  Pallas kernels  122 us (98%)
  local copies, waits for them, and re-layouts  2.73 us (2%)
    pallas_call x1, Pallas kernels, local(): pl.pallas_call(functools.partial(kernel, n, nh, cap), out_shape=jax.Shape...  122 us
    unnamed x1, local copies, waits for them, and re-layouts  2.73 us

profile of v5, /device:TPU:28, one launch (start us, length us, event | category | flops | bytes accessed | tf_op | source)
XLA Modules:
  0.0 125.0 jit_solution(4883269417794127275)
XLA Ops:
  0.0 122.2 %shard_map.73 = bf16[3,128,2048]{2,1,0:T(8,128)(2,1)} custom-call(bf16[128,2048]{1,0:T(8,128)(2,1)} %q_hbm.1, bf16[128,2048]{1,0:T(8,128)(2,1)} %k_hbm.1, bf16[128,2048]{1,0:T(8,128)(2,1)} %v_hbm.1, bf16[128,2048]{1,0:T(8,128)(2,1)} %gn_hbm.1, f32[1,2048]{1,0:T(1,128)} %bitcast.5, s32[1,128]{1,0:T(1,128)} %bitcast.6, s32[1,128]{1,0:T(1,128)} %bitcast.7), custom_call_target="tpu_custom_call" | custom-call | tf_op jit(solution)/shard_map/pallas_call | solution.py:473
  122.3 2.7 %copy.9 = bf16[128,3,2048]{2,0,1:T(8,128)(2,1)} copy(bf16[128,3,2048]{2,0,1:T(8,128)(2,1)} %bitcast.4) | data formatting | bytes 3145728

commit v6 on v4

--- a/solution.py
+++ b/solution.py
@@ -196,29 +196,6 @@
             def _():
                 far[(ahead - 1) * quarter : ahead * quarter, :] = jnp.zeros((quarter, HS), BF16)
 
-    def chain(scan, part):
-        own, arrived, total_ref, far, send, carry, leaving, entering, order, toward = scans[scan]
-        got_near(near_sems, scan, own, arrived, part)
-
-        @pl.when(gets(scan, 1))
-        def _():
-            copy_far(scan, total_ref, far, part, 1).wait_recv()
-
-        total = far[at_sub(0, part), :].astype(F32)
-        for block in order:
-            here = plane * PLANE + block
-            prior = doc(jnp.clip(here + toward, 0, n - 1), leaving)
-            send[at_sub(block, part), :] = (total * same(doc(here, entering), prior)).astype(BF16)
-            mine = arrived[at_sub(block, part), :].astype(F32)
-            total = mine + total * same(doc(here, leaving), prior)
-        total_ref[at_sub(0, part), :] = total.astype(BF16)
-
-        @pl.when(sends(scan, 1))
-        def _():
-            copy_far(scan, total_ref, far, part, 1).start()
-
-        send_near(carry_sems, scan, send, carry, part)
-
     def plane_total(scan, part):
         own, arrived, total_ref, far, _, _, leaving, _, order, toward = scans[scan]
         got_near(near_sems, scan, own, arrived, part)
@@ -314,7 +291,7 @@
     loop(SUBS // 2, inside)
     loop(n, pack)
     others(lambda other: copy_meta(other, other).wait_recv())
-    loop(SUBS, lambda part: chain(0, part))
+    loop(SUBS, lambda part: plane_total(0, part))
     loop(SUBS // 2, lambda part: inside(part + SUBS // 2))
 
     def unpack(source):
@@ -325,6 +302,7 @@
             jnp.where(row == lanes, 1.0, 0.0) * used
         ).astype(BF16)
 
+    loop(SUBS, lambda part: carries(0, part))
     loads[5].wait()
     loads[6].wait()
     if not aligned:
@@ -415,8 +393,8 @@
         bq_in[rows_at(group * n + me, cap), :] = bq_send[rows_at(group * n + me, cap), :]
 
     loop(half, lambda part: grad_query(0, part))
+    send_query(0)
     loop(SUBS, lambda part: plane_total(1, part))
-    send_query(0)
     loop(half, lambda part: grad_query(1, part))
     send_query(1)
 
@@ -481,7 +459,7 @@
         def drain(part):
             sent_near(near_sems, scan, own, arrived, part)
             sent_near(carry_sems, scan, send, carry, part)
-            for ahead in (1, 2)[: scan + 1]:
+            for ahead in (1, 2):
                 @pl.when(sends(scan, ahead))
                 def _():
                     copy_far(scan, total_ref, far, part, ahead).wait_send()

time: 117 us -> 118 us (level)
  the two profiles are of different devices: /device:TPU:0 before, /device:TPU:31 now
where the time goes in v6:
time: 118 us
  Pallas kernels  115 us (97%)
  local copies, waits for them, and re-layouts  2.73 us (2%)
    pallas_call x1, Pallas kernels, local(): pl.pallas_call(functools.partial(kernel, n, nh, cap), out_shape=jax.Shape...  115 us
    unnamed x1, local copies, waits for them, and re-layouts  2.73 us

profile of v6, /device:TPU:31, one launch (start us, length us, event | category | flops | bytes accessed | tf_op | source)
XLA Modules:
  0.0 118.2 jit_solution(6076239508720428823)
XLA Ops:
  0.0 115.5 %shard_map.73 = bf16[3,128,2048]{2,1,0:T(8,128)(2,1)} custom-call(bf16[128,2048]{1,0:T(8,128)(2,1)} %q_hbm.1, bf16[128,2048]{1,0:T(8,128)(2,1)} %k_hbm.1, bf16[128,2048]{1,0:T(8,128)(2,1)} %v_hbm.1, bf16[128,2048]{1,0:T(8,128)(2,1)} %gn_hbm.1, f32[1,2048]{1,0:T(1,128)} %bitcast.5, s32[1,128]{1,0:T(1,128)} %bitcast.6, s32[1,128]{1,0:T(1,128)} %bitcast.7), custom_call_target="tpu_custom_call" | custom-call | tf_op jit(solution)/shard_map/pallas_call | solution.py:492
  115.5 2.7 %copy.9 = bf16[128,3,2048]{2,0,1:T(8,128)(2,1)} copy(bf16[128,3,2048]{2,0,1:T(8,128)(2,1)} %bitcast.4) | data formatting | bytes 3145728

commit v7 on v6

--- a/solution.py
+++ b/solution.py
@@ -393,8 +393,8 @@
         bq_in[rows_at(group * n + me, cap), :] = bq_send[rows_at(group * n + me, cap), :]
 
     loop(half, lambda part: grad_query(0, part))
+    loop(SUBS, lambda part: plane_total(1, part))
     send_query(0)
-    loop(SUBS, lambda part: plane_total(1, part))
     loop(half, lambda part: grad_query(1, part))
     send_query(1)
 

time: 118 us -> 118 us (level)
  the two profiles are of different devices: /device:TPU:31 before, /device:TPU:0 now
where the time goes in v7:
time: 118 us; the launch traced here: 116 us
  Pallas kernels  113 us (96%)
  local copies, waits for them, and re-layouts  2.73 us (2%)
    pallas_call x1, Pallas kernels, local(): pl.pallas_call(functools.partial(kernel, n, nh, cap), out_shape=jax.Shape...  113 us
    unnamed x1, local copies, waits for them, and re-layouts  2.73 us

profile of v7, /device:TPU:0, one launch (start us, length us, event | category | flops | bytes accessed | tf_op | source)
XLA Modules:
  0.0 115.7 jit_solution(13122471164303039577)
XLA Ops:
  0.0 112.9 %shard_map.73 = bf16[3,128,2048]{2,1,0:T(8,128)(2,1)} custom-call(bf16[128,2048]{1,0:T(8,128)(2,1)} %q_hbm.1, bf16[128,2048]{1,0:T(8,128)(2,1)} %k_hbm.1, bf16[128,2048]{1,0:T(8,128)(2,1)} %v_hbm.1, bf16[128,2048]{1,0:T(8,128)(2,1)} %gn_hbm.1, f32[1,2048]{1,0:T(1,128)} %bitcast.5, s32[1,128]{1,0:T(1,128)} %bitcast.6, s32[1,128]{1,0:T(1,128)} %bitcast.7), custom_call_target="tpu_custom_call" | custom-call | tf_op jit(solution)/shard_map/pallas_call | solution.py:492
  113.0 2.7 %copy.9 = bf16[128,3,2048]{2,0,1:T(8,128)(2,1)} copy(bf16[128,3,2048]{2,0,1:T(8,128)(2,1)} %bitcast.4) | data formatting | bytes 3145728

commit v8 on v4

--- a/solution.py
+++ b/solution.py
@@ -12,6 +12,7 @@
 EPSILON = 1e-05
 PLANE = 4
 SUBS = 4
+STRIDE = 7
 F32 = jnp.float32
 BF16 = jnp.bfloat16
 
@@ -129,7 +130,7 @@
 
     def others(body):
         def step(index, _):
-            body(lax.rem(me + index, n))
+            body(lax.rem(me + STRIDE * index, n))
             return 0
 
         lax.fori_loop(1, n, step, 0)

time: 117 us -> 120 us (1.026)
  Pallas kernels: 113 us -> 115 us
    pallas_call x1, Pallas kernels: 113 us -> 115 us  [local(): pl.pallas_call(functools.partial(kernel, n, nh, cap), out_shape=jax.Shape...]
where the time goes in v8:
time: 120 us; the launch traced here: 118 us
  Pallas kernels  115 us (96%)
  local copies, waits for them, and re-layouts  2.73 us (2%)
    pallas_call x1, Pallas kernels, local(): pl.pallas_call(functools.partial(kernel, n, nh, cap), out_shape=jax.Shape...  115 us
    unnamed x1, local copies, waits for them, and re-layouts  2.73 us

profile of v8, /device:TPU:0, one launch (start us, length us, event | category | flops | bytes accessed | tf_op | source)
XLA Modules:
  0.0 117.5 jit_solution(17146016349191654641)
XLA Ops:
  0.0 114.8 %shard_map.73 = bf16[3,128,2048]{2,1,0:T(8,128)(2,1)} custom-call(bf16[128,2048]{1,0:T(8,128)(2,1)} %q_hbm.1, bf16[128,2048]{1,0:T(8,128)(2,1)} %k_hbm.1, bf16[128,2048]{1,0:T(8,128)(2,1)} %v_hbm.1, bf16[128,2048]{1,0:T(8,128)(2,1)} %gn_hbm.1, f32[1,2048]{1,0:T(1,128)} %bitcast.5, s32[1,128]{1,0:T(1,128)} %bitcast.6, s32[1,128]{1,0:T(1,128)} %bitcast.7), custom_call_target="tpu_custom_call" | custom-call | tf_op jit(solution)/shard_map/pallas_call | solution.py:515
  114.8 2.7 %copy.9 = bf16[128,3,2048]{2,0,1:T(8,128)(2,1)} copy(bf16[128,3,2048]{2,0,1:T(8,128)(2,1)} %bitcast.4) | data formatting | bytes 3145728

commit v9 on v4

--- a/solution.py
+++ b/solution.py
@@ -445,7 +445,14 @@
         bkv_send[rows_at(part, slots_all), :] = dot(
             pack_ref[...], jnp.concatenate(made[0] + made[1], axis=1), 1, 0
         ).astype(BF16)
-        others(lambda other: copy_rows(bkv_send, bkv_in, kv_sems, part, other, me).start())
+
+        def far_first(index, _):
+            away = (index + 1) // 2
+            other = lax.rem(me + n // 2 + away * (1 - 2 * lax.rem(index, 2)), n)
+            copy_rows(bkv_send, bkv_in, kv_sems, part, other, me).start()
+            return 0
+
+        lax.fori_loop(0, n - 1, far_first, 0)
         bkv_in[rows_at(part * n + me, cap), :] = bkv_send[rows_at(part * n + me, cap), :]
 
     loop(SUBS, grad_pair)

time: 117 us -> 119 us (1.017); the launches traced: 115 us -> 119 us
  Pallas kernels: 113 us -> 116 us
    pallas_call x1, Pallas kernels: 113 us -> 116 us  [local(): pl.pallas_call(functools.partial(kernel, n, nh, cap), out_shape=jax.Shape...]
where the time goes in v9:
time: 119 us
  Pallas kernels  116 us (97%)
  local copies, waits for them, and re-layouts  2.73 us (2%)
    pallas_call x1, Pallas kernels, local(): pl.pallas_call(functools.partial(kernel, n, nh, cap), out_shape=jax.Shape...  116 us
    unnamed x1, local copies, waits for them, and re-layouts  2.73 us

profile of v9, /device:TPU:0, one launch (start us, length us, event | category | flops | bytes accessed | tf_op | source)
XLA Modules:
  0.0 118.7 jit_solution(6150729681067658039)
XLA Ops:
  0.0 116.0 %shard_map.73 = bf16[3,128,2048]{2,1,0:T(8,128)(2,1)} custom-call(bf16[128,2048]{1,0:T(8,128)(2,1)} %q_hbm.1, bf16[128,2048]{1,0:T(8,128)(2,1)} %k_hbm.1, bf16[128,2048]{1,0:T(8,128)(2,1)} %v_hbm.1, bf16[128,2048]{1,0:T(8,128)(2,1)} %gn_hbm.1, f32[1,2048]{1,0:T(1,128)} %bitcast.5, s32[1,128]{1,0:T(1,128)} %bitcast.6, s32[1,128]{1,0:T(1,128)} %bitcast.7), custom_call_target="tpu_custom_call" | custom-call | tf_op jit(solution)/shard_map/pallas_call | solution.py:521
  116.0 2.7 %copy.9 = bf16[128,3,2048]{2,0,1:T(8,128)(2,1)} copy(bf16[128,3,2048]{2,0,1:T(8,128)(2,1)} %bitcast.4) | data formatting | bytes 3145728
